TPU v7x, 32 devices: a whole 2x2x4 slice. The times are simulated.
32 devices in a mesh: gy: 4 (over y, x), gx: 8 (over z, core).
Axes of the slice: x: 2, y: 2, z: 4, core: 2. Of those that a mesh axis runs over, the one named last changes fastest.
Arguments:
- ocean_state: bfloat16 [1536, 16, 2048], P('gy', None, 'gx'), may hold values from -6 to 6
- atm_blocks: bfloat16 [6144, 16, 128], P(('gy', 'gx')), may hold values from -6 to 6
- dest_tile: int32 [6144, 1], P(('gy', 'gx')), may hold values from 0 to 31; in each aligned block of 192 rows (0 to 191, 192 to 383, ...) at most 12 rows name the same one
- dest_row: int32 [6144], P(('gy', 'gx')), may hold values from 0 to 191
- live_entry: int32 [6144], P(('gy', 'gx')), may hold values 0 or 1
- land_mask: int32 [1536, 2048], P('gy', 'gx'), may hold values 0 or 1
- fold_pair: int32 [8], replicated, may hold values from 0 to 7, as said below
- first_weight: bfloat16 [3, 3, 64, 32], replicated, may hold values from -0.375 to 0.375
- first_bias: float32 [64], replicated, may hold values from -3 to 3
- second_weight: bfloat16 [3, 3, 8, 64], replicated, may hold values from -0.25 to 0.25
- second_bias: float32 [8], replicated, may hold values from -3 to 3
Outputs:
- eddy_forcing: bfloat16 [1536, 8, 2048], P('gy', None, 'gx')
Inputs may be any that keep to these rules, and one draw needn't show every extreme that they name: `dest_tile`: at most 12 of the 192 entries held by one device name the same tile, and some device names some tile exactly 12 times. fold_pair[fold_pair[t]] = t and fold_pair[t] != t for every tile t.
All inputs are finite; a program needn't handle non-finite values. No bound on the sum of `live_entry` or of `land_mask` on one device may be relied on, other than what follows from the above.
Results may differ from a plain program's by a relative error of at most 0.005.
Values may be sent and summed in bfloat16 or wider, within the bound.
A program may use at most 192 MiB of HBM per device.

v0:
```python
import jax
import jax.numpy as jnp
from jax import lax
from jax.sharding import PartitionSpec as P

row_block = 32


def with_halo(shard, sides, width, wrap):
    for axis, dim in sides:
        size, length = (lax.axis_size(axis), shard.shape[dim])
        up = [(i, (i + 1) % size) for i in range(size if wrap else size - 1)]
        down = [(j, i) for i, j in up]
        last = lax.slice_in_dim(shard, length - width, length, axis=dim)
        leading = lax.slice_in_dim(shard, 0, width, axis=dim)
        before = lax.ppermute(last, axis, up)
        after = lax.ppermute(leading, axis, down)
        shard = jnp.concatenate([before, shard, after], axis=dim)
    return shard


def fold_row(gathered, fold_pair, margin, signs):
    columns = gathered.shape[1]
    tile_count = fold_pair.shape[0]
    tile_cols = columns // tile_count
    placed = lax.axis_index("gx") * tile_cols + jnp.arange(
        -margin, tile_cols + margin, dtype=jnp.int32
    )
    placed = placed % columns
    tile_of = placed // tile_cols
    matches = tile_of[:, None] == jnp.arange(tile_count, dtype=jnp.int32)[None, :]
    partner_tile = jnp.sum(jnp.where(matches, fold_pair[None, :], 0), axis=1)
    partner = partner_tile * tile_cols + tile_cols - 1 - placed % tile_cols
    return jnp.take(gathered, partner, axis=1) * signs[:, None]


def convolve(padded, weight, finish):
    out_rows = padded.shape[0] - 2
    out_cols = padded.shape[2] - 2

    def block_out(start, count):
        piece = lax.dynamic_slice_in_dim(padded, start, count + 2, 0)
        total = jnp.zeros((count, weight.shape[2], out_cols), jnp.float32)
        for shift_y in range(3):
            for shift_x in range(3):
                total = total + jnp.einsum(
                    "oc,ycx->yox",
                    weight[shift_y, shift_x],
                    piece[shift_y : shift_y + count, :, shift_x : shift_x + out_cols],
                    preferred_element_type=jnp.float32,
                )
        return finish(total, start, count)

    whole_blocks = out_rows // row_block
    mapped = lax.map(
        lambda number: block_out(number * row_block, row_block),
        jnp.arange(whole_blocks, dtype=jnp.int32),
    )
    pieces = mapped.reshape((whole_blocks * row_block,) + mapped.shape[2:])
    return pieces


def per_device(
    ocean_state,
    atm_blocks,
    dest_tile,
    dest_row,
    live_entry,
    land_mask,
    fold_pair,
    first_weight,
    first_bias,
    second_weight,
    second_bias,
):
    tile_rows = ocean_state.shape[0]
    half_rows = tile_rows // 2
    fields = atm_blocks.shape[1]
    block_cols = atm_blocks.shape[2]
    held = atm_blocks.shape[0]
    lat_tiles = lax.axis_size("gy")
    lon_tiles = lax.axis_size("gx")
    devices = lat_tiles * lon_tiles
    capacity = max(2, 2 * held // devices)
    targets = dest_tile[:, 0]
    is_live = live_entry == 1
    hits = (
        (targets[:, None] == jnp.arange(devices, dtype=jnp.int32)[None, :]) & is_live[:, None]
    ).astype(jnp.int32)
    earlier = jnp.cumsum(hits, axis=0) - hits
    ranks = jnp.sum(earlier * hits, axis=1)
    placing = jnp.where(is_live, targets * capacity + ranks, devices * capacity)
    outgoing = (
        jnp.zeros((devices * capacity, fields, block_cols), jnp.bfloat16)
        .at[placing]
        .set(atm_blocks, mode="drop")
    )
    outgoing_rows = (
        jnp.full((devices * capacity,), -1, jnp.int32).at[placing].set(dest_row, mode="drop")
    )
    incoming, incoming_rows = (
        lax.all_to_all(
            outgoing.reshape(devices, capacity, fields, block_cols),
            ("gy", "gx"),
            split_axis=0,
            concat_axis=0,
            tiled=True,
        ),
        lax.all_to_all(
            outgoing_rows.reshape(devices, capacity),
            ("gy", "gx"),
            split_axis=0,
            concat_axis=0,
            tiled=True,
        ),
    )
    selector = (
        incoming_rows.reshape(1, -1) == jnp.arange(half_rows, dtype=jnp.int32)[:, None]
    ).astype(jnp.bfloat16)
    coarse = jnp.dot(
        selector, incoming.reshape(-1, fields * block_cols), preferred_element_type=jnp.float32
    ).astype(jnp.bfloat16)
    coarse = coarse.reshape(half_rows, fields, block_cols)
    forcing = jnp.repeat(jnp.repeat(coarse, 2, axis=0), 2, axis=2)
    mask_values = land_mask.astype(jnp.bfloat16)[:, None, :]
    inputs = jnp.concatenate([ocean_state, forcing], axis=1) * mask_values
    levels = ocean_state.shape[1] // 4
    channel = jnp.arange(inputs.shape[1])
    in_signs = jnp.where(
        (channel < 2 * levels) | (channel == 4 * levels) | (channel == 4 * levels + 1), -1.0, 1.0
    ).astype(jnp.bfloat16)
    is_top = lax.axis_index("gy") == lat_tiles - 1
    top_inputs = lax.all_gather(inputs[-1], "gx", axis=1, tiled=True)

    def hidden_finish(total, start, count):
        return jnp.maximum(total + first_bias[None, :, None], 0.0).astype(jnp.bfloat16)

    sides = with_halo(inputs, (("gx", 2),), 1, True)
    padded = with_halo(sides, (("gy", 0),), 1, False)
    folded = fold_row(top_inputs, fold_pair, 1, in_signs)
    padded = padded.at[tile_rows + 1].set(jnp.where(is_top, folded, padded[tile_rows + 1]))
    hidden = convolve(padded, first_weight, hidden_finish)
    top_hidden = hidden[-1]
    gathered_hidden = lax.all_gather(top_hidden, "gx", axis=1, tiled=True)
    hidden_signs = jnp.ones((first_weight.shape[2],), jnp.bfloat16)
    hidden_folded = fold_row(gathered_hidden, fold_pair, 1, hidden_signs)
    hidden_sides = with_halo(hidden, (("gx", 2),), 1, True)
    padded_hidden = with_halo(hidden_sides, (("gy", 0),), 1, False)
    padded_hidden = padded_hidden.at[tile_rows + 1].set(
        jnp.where(is_top, hidden_folded, padded_hidden[tile_rows + 1])
    )

    def output_finish(total, start, count):
        mask_rows = lax.dynamic_slice_in_dim(mask_values, start, count, 0)
        return ((total + second_bias[None, :, None]) * mask_rows).astype(jnp.bfloat16)

    return convolve(padded_hidden, second_weight, output_finish)


def solution(mesh):
    return jax.shard_map(
        per_device,
        mesh=mesh,
        in_specs=(
            P("gy", None, "gx"),
            P(("gy", "gx"), None, None),
            P(("gy", "gx"), None),
            P(("gy", "gx")),
            P(("gy", "gx")),
            P("gy", "gx"),
            P(),
            P(),
            P(),
            P(),
            P(),
        ),
        out_specs=P("gy", None, "gx"),
        check_vma=False,
    )
```

profile of v0, /device:TPU:6, one launch (start us, length us, event | category | flops | bytes accessed | tf_op | source)
XLA Modules:
  0.0 810.6 jit_solution(16251035017874326998)
XLA Ops:
  5.8 6.1 all-to-all-start
  13.2 21.2 %scatter_fusion = bf16[384,16,128]{2,1,0:T(8,128)(2,1)} fusion(bf16[384,16,128]{2,1,0:T(8,128)(2,1)} %broadcast_in_dim.98, s32[192]{0:T(256)S(1)} %compare_select_fusion.6, bf16[192,16,128]{2,1,0:T(8,128)(2,1)} %param.20), kind=kCustom, calls=%fused_computation.3 | custom fusion | bytes 2360064 | tf_op jit(solution)/shard_map/scatter | solution.py:96
  34.5 5.9 all-to-all-start.1
  40.4 17.7 %copy.114 = bf16[384,16,256]{1,2,0:T(8,128)(2,1)} copy(bf16[384,16,256]{2,1,0:T(8,128)(2,1)} %param.19) | data formatting | bytes 6291456 | tf_op args[0]
  60.3 16.8 %all-to-all-done.1 = bf16[32,12,16,128]{3,2,1,0:T(8,128)(2,1)S(1)} async-done(((bf16[32,12,16,128]{3,2,1,0:T(8,128)(2,1)}), bf16[32,12,16,128]{3,2,1,0:T(8,128)(2,1)S(1)}, u32[]{:S(2)}, u32[]{:S(2)}) %all-to-all-start.1) | async-done | bytes 1572896 | tf_op jit(solution)/shard_map/all_to_all | solution.py:102
  82.1 19.3 %copy.115 = bf16[384,16,256]{1,2,0:T(8,128)(2,1)} copy(bf16[384,16,256]{0,1,2:T(8,128)(2,1)S(1)} %bitcast.206) | data formatting | bytes 6291456 | tf_op jit(solution)/shard_map/reshape | solution.py:124
  101.4 24.9 %maximum_multiply_fusion = bf16[384,32,256]{1,2,0:T(8,128)(2,1)} fusion(bf16[384,16,256]{1,2,0:T(8,128)(2,1)} %copy.115, bf16[384,16,256]{1,2,0:T(8,128)(2,1)} %copy.114, bf16[384,256]{1,0:T(8,128)(2,1)} %convert_element_type.27), kind=kLoop, calls=%fused_computation.104 | loop fusion | flops 18874368 | bytes 12779520 | tf_op jit(solution)/shard_map/mul | solution.py:126
  131.6 5.1 collective-permute-done
  136.8 16.4 %pad_maximum_fusion.1 = bf16[384,32,258]{1,2,0:T(8,128)(2,1)S(1)} fusion(bf16[384,32,1]{1,2,0:T(2,128)(2,1)S(1)} %collective-permute-done.1, bf16[384,32,256]{1,2,0:T(8,128)(2,1)} %maximum_multiply_fusion, bf16[384,32,1]{1,2,0:T(2,128)(2,1)S(1)} %collective-permute-done), kind=kLoop, calls=%fused_computation.103 | loop fusion | flops 19021824 | bytes 12681216 | tf_op jit(solution)/shard_map/concatenate | solution.py:18
  153.2 8.6 %copy-done = bf16[384,32,258]{1,2,0:T(8,128)(2,1)} copy-done((bf16[384,32,258]{1,2,0:T(8,128)(2,1)}, bf16[384,32,258]{1,2,0:T(8,128)(2,1)S(1)}, u32[]{:S(2)}) %copy-start) | copy-done | bytes 6340632
  164.9 14.7 %all-gather = bf16[1,32,2048]{1,2,0:T(8,128)(2,1)S(1)} all-gather(bf16[1,32,256]{1,2,0:T(8,128)(2,1)S(1)} %slice-done), channel_id=2, replica_groups=mesh['gy'=4,'gx'=8] {'gx'}, dimensions={2}, use_global_device_ids=true | all-gather | bytes 147456 | tf_op jit(solution)/shard_map/all_gather | solution.py:133
  181.0 33.0 %copy.118 = bf16[384,32,258]{0,1,2:T(8,128)(2,1)} copy(bf16[384,32,258]{1,2,0:T(8,128)(2,1)} %copy-done) | data formatting | bytes 12681216 | tf_op jit(solution)/shard_map/concatenate | solution.py:18
  224.5 9.6 %pad_maximum_fusion.2 = bf16[386,32,258]{0,1,2:T(8,128)(2,1)} fusion(bf16[1,32,258]{0,1,2:T(8,128)(2,1)S(1)} %copy.119, bf16[384,32,258]{0,1,2:T(8,128)(2,1)} %copy.118, bf16[1,32,258]{0,1,2:T(8,128)(2,1)} %copy.117), kind=kLoop, calls=%fused_computation.105 | loop fusion | flops 19120896 | bytes 12747264 | tf_op jit(solution)/shard_map/concatenate | solution.py:18
  234.1 25.1 %scatter.26 = bf16[386,32,258]{0,1,2:T(8,128)(2,1)} dynamic-update-slice(bf16[386,32,258]{0,1,2:T(8,128)(2,1)} %pad_maximum_fusion.2, bf16[1,32,258]{0,1,2:T(8,128)(2,1)} %copy.120, s32[]{:T(128)} %constant.197.clone.1, s32[]{:T(128)} %constant.177.clone.1, s32[]{:T(128)} %constant.177.clone.1) | dynamic-update-slice | bytes 33028 | tf_op jit(solution)/shard_map/scatter | solution.py:141
  259.2 15.9 %copy.121 = bf16[386,32,258]{2,1,0:T(8,128)(2,1)} copy(bf16[386,32,258]{0,1,2:T(8,128)(2,1)} %scatter.26) | data formatting | bytes 12747264 | tf_op jit(solution)/shard_map/while | solution.py:55
  275.2 212.2 %while.22 = (s32[]{:T(128)}, bf16[12,32,64,256]{3,2,1,0:T(8,128)(2,1)}, s32[12]{0:T(128)S(1)}, bf16[386,32,258]{2,1,0:T(8,128)(2,1)}, bf16[3,3,64,32]{2,3,1,0:T(...) while((s32[]{:T(128)}, ...), condition=%wide.region_7.8_spmd, body=%wide.region_6.7_spmd.sunk | while | flops 307757056 | bytes 39396632 | solution.py:55
  377.6 3.7 fusion.188
  487.4 22.8 %copy.122 = bf16[12,32,64,256]{2,3,1,0:T(8,128)(2,1)} copy(bf16[12,32,64,256]{3,2,1,0:T(8,128)(2,1)} %get-tuple-element.98) | data formatting | bytes 25165824 | tf_op jit(solution)/shard_map/while | solution.py:55
  516.4 3.7 collective-permute-done.4
  522.4 5.2 collective-permute-start.7
  527.6 14.9 %all-gather.1 = bf16[1,64,2048]{1,2,0:T(8,128)(2,1)S(1)} all-gather(bf16[1,64,256]{1,2,0:T(8,128)(2,1)S(1)} %slice.213), channel_id=3, replica_groups=mesh['gy'=4,'gx'=8] {'gx'}, dimensions={2}, use_global_device_ids=true | all-gather | bytes 294912 | tf_op jit(solution)/shard_map/all_gather | solution.py:144
  544.0 24.6 %pad_maximum_fusion = bf16[386,64,258]{1,2,0:T(8,128)(2,1)} fusion(bf16[1,64,258]{1,2,0:T(8,128)(2,1)S(1)} %collective-permute-done.7, bf16[384,64,1]{1,2,0:T(2,128)(2,1)S(1)} %collective-permute-done.5, bf16[384,64,256]{1,2,0:T(8,128)(2,1)} %bitcast.205, bf16[384,64,1]{1,2,0:T(2,128)(2,1)S(1)} %collective-permute-done.4, bf16[1,64,258]{1,2,0:T(8,128)(2,1)S(1)} %copy.124), kind=kLoop, calls=%fused_computation.102 | loop fusion | flops 63736320 | bytes 25494528 | tf_op jit(solution)/shard_map/concatenate | solution.py:18
  569.3 29.0 %copy.125 = bf16[386,64,258]{2,1,0:T(8,128)(2,1)} copy(bf16[386,64,258]{1,2,0:T(8,128)(2,1)} %fusion.95) | data formatting | bytes 25494528 | tf_op jit(solution)/shard_map/while | solution.py:55
  598.4 212.3 %while.23 = (s32[]{:T(128)}, bf16[12,32,8,256]{3,2,1,0:T(8,128)(2,1)}, s32[12]{0:T(128)S(1)}, bf16[386,64,258]{2,1,0:T(8,128)(2,1)}, bf16[3,3,8,64]{3,2,1,0:T(8,...) while((s32[]{:T(128)}, ...), condition=%wide.region_9.10_spmd, body=%wide.region_8.9_spmd.sunk | while | flops 76226568 | bytes 13864264 | solution.py:55
  (329 shorter events, 451.8 us)
Async XLA Ops:
  5.8 28.7 %all-to-all-start = ((s32[32,1,12]{2,1,0:T(1,128)}), s32[32,1,12]{2,1,0:T(1,128)S(1)}, u32[]{:S(2)}, u32[]{:S(2)}) async-start(s32[32,1,12]{2,1,0:T(1,128)} %bitcast.45), calls=%async_computation | async-start | bytes 32768 | tf_op jit(solution)/shard_map/all_to_all | solution.py:109
  34.5 42.6 %all-to-all-start.1 = ((bf16[32,12,16,128]{3,2,1,0:T(8,128)(2,1)}), bf16[32,12,16,128]{3,2,1,0:T(8,128)(2,1)S(1)}, u32[]{:S(2)}, u32[]{:S(2)}) async-start(bf16[32,12,16,128]{3,2,1,0:T(8,128)(2,1)} %bitcast.46), calls=%async_computation.1 | async-start | bytes 3145728 | tf_op jit(solution)/shard_map/all_to_all | solution.py:102
  40.4 17.7 %copy-start.2 = (s32[384,256]{1,0:T(8,128)S(1)}, s32[384,256]{1,0:T(8,128)}, u32[]{:S(2)}) copy-start(s32[384,256]{1,0:T(8,128)} %param.24) | copy-start | bytes 1179652
  40.4 18.4 %copy-start.6 = (s32[8]{0:T(128)S(1)}, s32[8]{0:T(128)}, u32[]{:S(2)}) copy-start(s32[8]{0:T(128)} %param.25) | copy-start | bytes 100
  128.0 8.7 %collective-permute-start = (bf16[384,32,1]{1,2,0:T(2,128)(2,1)S(1)}, bf16[384,32,1]{1,2,0:T(2,128)(2,1)S(1)}, u32[]{:S(2)}, u32[]{:S(2)}) collective-permute-start(bf16[384,32,1]{1,2,0:T(2,128)(2,1)S(1)} %get-tuple-element.223), channel_id=1, source_target_pairs={{0,1},{1,2},{2,3},{3,4},{4,5},{5,6},{6,7},{7,0},{8,9},{9,10},{10,1... | collective-permute-start | bytes 73736 | tf_op jit(solution)/shard_map/ppermute | solution.py:16
  128.4 8.4 %collective-permute-start.1 = (bf16[384,32,1]{1,2,0:T(2,128)(2,1)S(1)}, bf16[384,32,1]{1,2,0:T(2,128)(2,1)S(1)}, u32[]{:S(2)}, u32[]{:S(2)}) collective-permute-start(bf16[384,32,1]{1,2,0:T(2,128)(2,1)S(1)} %get-tuple-element.224), channel_id=1, source_target_pairs={{1,0},{2,1},{3,2},{4,3},{5,4},{6,5},{7,6},{0,7},{9,8},{10,9},{11,1... | collective-permute-start | bytes 73736 | tf_op jit(solution)/shard_map/ppermute | solution.py:17
  131.6 33.3 %slice-start = ((bf16[384,32,256]{1,2,0:T(8,128)(2,1)}), bf16[1,32,256]{1,2,0:T(8,128)(2,1)S(1)}, s32[]{:S(2)}) async-start(bf16[384,32,256]{1,2,0:T(8,128)(2,1)} %maximum_multiply_fusion), calls=%async_computation.2 | async-start | bytes 131072 | tf_op jit(solution)/shard_map/slice | solution.py:133
  153.2 8.6 %copy-start = (bf16[384,32,258]{1,2,0:T(8,128)(2,1)}, bf16[384,32,258]{1,2,0:T(8,128)(2,1)S(1)}, u32[]{:S(2)}) copy-start(bf16[384,32,258]{1,2,0:T(8,128)(2,1)S(1)} %pad_maximum_fusion.1) | copy-start | bytes 19021828
  161.7 53.8 %collective-permute-start.3 = (bf16[1,32,258]{1,2,0:T(8,128)(2,1)S(1)}, bf16[1,32,258]{1,2,0:T(8,128)(2,1)S(1)}, u32[]{:S(2)}, u32[]{:S(2)}) collective-permute-start(bf16[1,32,258]{1,2,0:T(8,128)(2,1)S(1)} %get-tuple-element.218), channel_id=1, source_target_pairs={{8,0},{16,8},{24,16},{9,1},{17,9},{25,17},{10,2},{18,10},{26,18},{... | collective-permute-start | bytes 49544 | tf_op jit(solution)/shard_map/ppermute | solution.py:17
  214.1 7.2 collective-permute-start.2
  259.2 16.0 %copy-start.1 = (bf16[3,3,64,32]{2,3,1,0:T(8,128)(2,1)S(1)}, bf16[3,3,64,32]{2,3,1,0:T(8,128)(2,1)}, u32[]{:S(2)}) copy-start(bf16[3,3,64,32]{2,3,1,0:T(8,128)(2,1)} %param.26) | copy-start | bytes 110596
  259.2 16.0 %copy-start.4 = (f32[64]{0:T(128)S(1)}, f32[64]{0:T(128)}, u32[]{:S(2)}) copy-start(f32[64]{0:T(128)} %param.27) | copy-start | bytes 772
  511.9 8.2 %collective-permute-start.4 = (bf16[384,64,1]{1,2,0:T(2,128)(2,1)S(1)}, bf16[384,64,1]{1,2,0:T(2,128)(2,1)S(1)}, u32[]{:S(2)}, u32[]{:S(2)}) collective-permute-start(bf16[384,64,1]{1,2,0:T(2,128)(2,1)S(1)} %get-tuple-element.221), channel_id=1, source_target_pairs={{0,1},{1,2},{2,3},{3,4},{4,5},{5,6},{6,7},{7,0},{8,9},{9,10},{10,1... | collective-permute-start | bytes 147464 | tf_op jit(solution)/shard_map/ppermute | solution.py:16
  512.3 7.8 collective-permute-start.5
  521.1 22.8 %collective-permute-start.6 = (bf16[1,64,258]{2,1,0:T(8,128)(2,1)S(1)}, bf16[1,64,258]{2,1,0:T(8,128)(2,1)S(1)}, u32[]{:S(2)}, u32[]{:S(2)}) collective-permute-start(bf16[1,64,258]{2,1,0:T(8,128)(2,1)S(1)} %copy.123), channel_id=1, source_target_pairs={{0,8},{8,16},{16,24},{1,9},{9,17},{17,25},{2,10},{10,18},{18,26},{... | collective-permute-start | bytes 99080 | tf_op jit(solution)/shard_map/ppermute | solution.py:16
  522.4 21.6 %collective-permute-start.7 = (bf16[1,64,258]{1,2,0:T(8,128)(2,1)S(1)}, bf16[1,64,258]{1,2,0:T(8,128)(2,1)S(1)}, u32[]{:S(2)}, u32[]{:S(2)}) collective-permute-start(bf16[1,64,258]{1,2,0:T(8,128)(2,1)S(1)} %get-tuple-element.220), channel_id=1, source_target_pairs={{8,0},{16,8},{24,16},{9,1},{17,9},{25,17},{10,2},{18,10},{26,18},{... | collective-permute-start | bytes 99080 | tf_op jit(solution)/shard_map/ppermute | solution.py:17
  569.3 29.0 %copy-start.3 = (bf16[3,3,8,64]{3,2,1,0:T(8,128)(2,1)S(1)}, bf16[3,3,8,64]{3,2,1,0:T(8,128)(2,1)}, u32[]{:S(2)}) copy-start(bf16[3,3,8,64]{3,2,1,0:T(8,128)(2,1)} %param.28) | copy-start | bytes 27652
  569.3 29.0 %copy-start.5 = (f32[8]{0:T(128)S(1)}, f32[8]{0:T(128)}, u32[]{:S(2)}) copy-start(f32[8]{0:T(128)} %param.29) | copy-start | bytes 100
where the time goes:
time: 826 us; the launch traced here: 811 us
  matrix products  397 us (48%)
  local copies, waits for them, and re-layouts  231 us (28%)
  other arithmetic  82.3 us (10%)
  starting transfers between devices  30.3 us (4%)
  blocking collectives  29.6 us (4%)
  waiting for transfers between devices  25.7 us (3%)
  loops' own time  14.3 us (2%)
    dot_general x216, matrix products, block_out(): jnp.einsum('oc,ycx->yox', weight[shift_y, shift_x], piece[shift_y:shift_y...  396 us
    while x3, local copies, waits for them, and re-layouts, convolve(): lax.map(lambda number: block_out(number * row_block, row_block), jnp.aran...  67.8 us
    concatenate x3, other arithmetic, with_halo(): shard = jnp.concatenate([before, shard, after], axis=dim)  50.5 us
    concatenate x1, local copies, waits for them, and re-layouts, with_halo(): shard = jnp.concatenate([before, shard, after], axis=dim)  33 us
    unnamed x16, local copies, waits for them, and re-layouts  26.4 us
    scatter x1, local copies, waits for them, and re-layouts, per_device(): padded.at[tile_rows + 1]  25.1 us
    mul x1, other arithmetic, per_device(): inputs = jnp.concatenate([ocean_state, forcing], axis=1) * mask_values  24.9 us
    reshape x2, local copies, waits for them, and re-layouts, per_device(): forcing = jnp.repeat(jnp.repeat(coarse, 2, axis=0), 2, axis=2)  21.7 us
  transfers between devices with their start and end apart: 10, of which 3 were waited for; matrix products, arithmetic and copies ran while one was open for 10% of the time, Pallas kernels for 0%

commit v1 on v0

v1 whole, which is shorter than its diff:
```python
import functools

import jax
import jax.numpy as jnp
import numpy as np
from jax import lax
from jax.experimental import pallas as pl
from jax.experimental.pallas import tpu as pltpu
from jax.sharding import PartitionSpec as P

MESH = pl.DeviceIdType.MESH
R1 = 6
R2 = 6
f32 = jnp.float32
bf16 = jnp.bfloat16


def vmem():
    return pl.BlockSpec(memory_space=pltpu.VMEM)


def smem():
    return pl.BlockSpec(memory_space=pltpu.SMEM)


def anym():
    return pl.BlockSpec(memory_space=pl.ANY)


def pack_kernel(cap, tile_ref, row_ref, live_ref, atm_ref, out_ref, rows_ref, count):
    devices = count.shape[0]

    def clear(i, _):
        count[i] = 0
        return 0

    def clear_rows(i, _):
        rows_ref[i] = -1
        return 0

    lax.fori_loop(0, devices, clear, 0)
    lax.fori_loop(0, rows_ref.shape[0], clear_rows, 0, unroll=8)

    def place(e, _):
        @pl.when(live_ref[e] == 1)
        def _():
            t = tile_ref[e]
            c = count[t]
            count[t] = c + 1
            slot = t * cap + c
            rows_ref[slot] = row_ref[e]
            out_ref[slot] = atm_ref[e]

        return 0

    lax.fori_loop(0, atm_ref.shape[0], place, 0)


def combine_kernel(rows_ref, blocks_ref, state_ref, mask_ref, up_ref, inp_ref, cols_ref, acc, up):
    half = acc.shape[0]
    tile_rows, levels = state_ref.shape[0], state_ref.shape[1]
    acc[...] = jnp.zeros_like(acc)

    def add(s, _):
        r = rows_ref[s]

        @pl.when(r >= 0)
        def _():
            acc[r] += blocks_ref[s].astype(f32)

        return 0

    lax.fori_loop(0, rows_ref.shape[0], add, 0, unroll=4)

    def spread(i, _):
        piece = acc[pl.ds(i * 8, 8)].astype(bf16).reshape(8 * 16, 128)
        wide = jnp.dot(piece, up_ref[...], preferred_element_type=f32)
        up[pl.ds(i * 8, 8)] = wide.reshape(8, 16, 256)
        return 0

    lax.fori_loop(0, half // 8, spread, 0)

    lane = lax.broadcasted_iota(jnp.int32, (32, 128), 1)

    def rows8(i, carry):
        lo, hi = carry
        m = mask_ref[pl.ds(i * 8, 8), :].astype(f32)
        for k in range(8):
            y = i * 8 + k
            mk = jnp.broadcast_to(m[k : k + 1, :], (16, 256))
            a = state_ref[y].astype(f32) * mk
            b = up[i * 4 + k // 2] * mk
            full = jnp.concatenate([a, b], axis=0)
            inp_ref[y] = full.astype(bf16)
            at = lax.rem(2 * y, 128)
            here = (lane >> 1) == lax.rem(y, 64)
            lo = jnp.where(here, pltpu.roll(full[:, :128], at, 1), lo)
            hi = jnp.where(here, pltpu.roll(full[:, 128:], lax.rem(at + 2, 128), 1), hi)
        return lo, hi

    zero = jnp.zeros((32, 128), f32)

    def tile(t, _):
        lo, hi = lax.fori_loop(t * 8, t * 8 + 8, rows8, (zero, zero))
        cols_ref[0, t] = lo.astype(bf16)
        cols_ref[1, t] = hi.astype(bf16)
        return 0

    lax.fori_loop(0, tile_rows // 64, tile, 0)


def exchange_kernel(g_y, g_x, cols_ref, inp_ref, from_cols, rows_s, rows_n, top_all, send, recv, own):
    gy, gx = lax.axis_index("gy"), lax.axis_index("gx")
    n_rows = inp_ref.shape[0]
    west, east = lax.rem(gx + g_x - 1, g_x), lax.rem(gx + 1, g_x)
    low, high = inp_ref.at[pl.ds(0, 2)], inp_ref.at[pl.ds(n_rows - 2, 2)]
    is_top = gy == g_y - 1
    barrier = pltpu.get_barrier_semaphore()

    def copy(src, dst, s, r, y, x):
        return pltpu.make_async_remote_copy(
            src_ref=src, dst_ref=dst, send_sem=send.at[s], recv_sem=recv.at[r], device_id=(y, x), device_id_type=MESH
        )

    def signal(y, x):
        pl.semaphore_signal(barrier, inc=1, device_id=(y, x), device_id_type=MESH)

    sides = (west, gx, east)

    @pl.when(gy > 0)
    def _():
        for x in sides:
            signal(gy - 1, x)

    @pl.when(gy < g_y - 1)
    def _():
        for x in sides:
            signal(gy + 1, x)
        for x in (west, east):
            signal(gy, x)

    @pl.when(is_top)
    def _():
        def one(d, _):
            signal(gy, lax.rem(gx + d, g_x))
            return 0

        lax.fori_loop(1, g_x, one, 0)

    top, bottom = is_top.astype(jnp.int32), (gy == 0).astype(jnp.int32)
    pl.semaphore_wait(barrier, top * (g_x - 1) + (1 - top) * 5 + (1 - bottom) * 3)

    to_west = copy(cols_ref.at[0], from_cols.at[1], 0, 1, gy, west)
    to_east = copy(cols_ref.at[1], from_cols.at[0], 1, 0, gy, east)
    to_south = [copy(low, rows_n.at[2 - k], 2 + k, 5 + 2 - k, gy - 1, sides[k]) for k in range(3)]
    to_north = [copy(high, rows_s.at[2 - k], 5 + k, 2 + 2 - k, gy + 1, sides[k]) for k in range(3)]
    mine = pltpu.make_async_copy(high, top_all.at[gx], own)

    def top_copy(d):
        return copy(high, top_all.at[gx], 8 + d, 8 + d, gy, lax.rem(gx + d, g_x))

    @pl.when(is_top)
    def _():
        def one(d, _):
            top_copy(d).start()
            return 0

        mine.start()
        lax.fori_loop(1, g_x, one, 0)

    @pl.when(gy > 0)
    def _():
        for c in to_south:
            c.start()

    @pl.when(gy < g_y - 1)
    def _():
        for c in to_north:
            c.start()

    to_west.start()
    to_east.start()
    to_west.wait()
    to_east.wait()

    @pl.when(gy > 0)
    def _():
        for c in to_south:
            c.wait_send()
        for k in range(3):
            copy(high, rows_s.at[k], 5, 2 + k, gy, west).wait_recv()

    @pl.when(gy < g_y - 1)
    def _():
        for c in to_north:
            c.wait_send()
        for k in range(3):
            copy(low, rows_n.at[k], 2, 5 + k, gy, west).wait_recv()

    @pl.when(is_top)
    def _():
        def one(d, _):
            c = top_copy(d)
            c.wait_send()
            src = lax.rem(gx + g_x - d, g_x)
            copy(high, top_all.at[src], 8 + d, 8 + d, gy, src).wait_recv()
            return 0

        lax.fori_loop(1, g_x, one, 0)
        mine.wait()


def roll(x, shift, axis=1):
    if isinstance(shift, int):
        shift = shift % x.shape[axis]
        if shift == 0:
            return x
    return pltpu.roll(x, shift, axis)


def conv_kernel(
    g_y, g_x, fold_ref, inp_ref, cols_ref, from_ref, rs_ref, rn_ref, top_ref, mask_ref, w1_ref, w1s_ref, b1_ref, w2_ref,
    w2e_ref, b2_ref, sign_ref, out_ref, x_ref, xl_ref, xr_ref, h_ref, north, south, edge, pedge, sem,
):
    gy, gx = lax.axis_index("gy"), lax.axis_index("gx")
    rows = out_ref.shape[0]
    hid = w1s_ref.shape[0]
    is_top = gy == g_y - 1
    load = pltpu.make_async_copy(inp_ref, x_ref.at[pl.ds(2, rows)], sem)
    load.start()
    lane256 = lax.broadcasted_iota(jnp.int32, (32, 256), 1)
    lane128 = lax.broadcasted_iota(jnp.int32, (32, 128), 1)
    back = (
        lax.broadcasted_iota(jnp.int32, (256, 256), 0) + lax.broadcasted_iota(jnp.int32, (256, 256), 1) == 255
    ).astype(bf16)

    def mirror(v):
        return jnp.dot(v, back, preferred_element_type=f32)

    def top_row(t):
        return mirror(top_ref[t, 1]) * sign_ref[...]

    def put(x, west, east):
        left = jnp.where(lane256 == 0, jnp.concatenate([west, west], axis=1), roll(x, 1))
        right = jnp.where(lane256 == 255, jnp.concatenate([east, east], axis=1), roll(x, -1))
        return left, right

    def side_rows(first, mid, last):
        return put(mid, roll(first[:, 128:], 1), roll(last[:, :128], -1))

    for j in range(2):
        for k in range(3):
            south[k, j] = jnp.where(gy > 0, rs_ref[k, j].astype(f32), 0.0)

    @pl.when(jnp.logical_not(is_top))
    def _():
        for j in range(2):
            for k in range(3):
                north[k, j] = rn_ref[k, j].astype(f32)

    @pl.when(is_top)
    def _():
        for k in range(3):
            t = fold_ref[lax.rem(gx + g_x - 1 + k, g_x)]
            north[k, 0] = top_row(t)
            north[k, 1] = jnp.zeros((32, 256), f32)

    def ext_hi(r0, r1, s0, s1):
        return jnp.where(lane128 >= 126, r1, roll(r0, -2)), jnp.where(lane128 < 2, roll(s0, 2), roll(s1, 4))

    def ext_lo(r0, r1, s0, s1):
        return jnp.where(lane128 >= 126, roll(r1, 126), roll(r0, 124)), jnp.where(lane128 < 2, s0, roll(s1, 2))

    def strip(body, ends):
        first, last = ends
        return jnp.concatenate([first] + [body[t].astype(f32) for t in range(rows // 64)] + [last], axis=1)

    hi, lo = slice(128, 256), slice(0, 128)
    far_w = strip(from_ref.at[0], ext_hi(south[0, 0][:, hi], south[0, 1][:, hi], north[0, 0][:, hi], north[0, 1][:, hi]))
    own_w = strip(cols_ref.at[0], ext_lo(south[1, 0][:, lo], south[1, 1][:, lo], north[1, 0][:, lo], north[1, 1][:, lo]))
    own_e = strip(cols_ref.at[1], ext_hi(south[1, 0][:, hi], south[1, 1][:, hi], north[1, 0][:, hi], north[1, 1][:, hi]))
    far_e = strip(from_ref.at[1], ext_lo(south[2, 0][:, lo], south[2, 1][:, lo], north[2, 0][:, lo], north[2, 1][:, lo]))

    def hidden_of(parts):
        stack = jnp.concatenate([p.astype(bf16) for p in parts], axis=0)
        total = jnp.dot(w1s_ref[...], stack, preferred_element_type=f32)
        return jnp.maximum(total + b1_ref[...], 0.0)

    west_parts, east_parts = [], []
    for u in range(3):
        s = -2 * (u - 1)
        west_parts += [roll(far_w, s), roll(far_w, s - 1), roll(own_w, s)]
        east_parts += [roll(own_e, s - 1), roll(far_e, s), roll(far_e, s - 1)]
    edge_lane = lax.broadcasted_iota(jnp.int32, (hid, 128 * (rows // 64 + 2)), 1)
    live = (edge_lane >= 128) | (gy > 0)
    edge[0] = jnp.where(live, hidden_of(west_parts), 0.0)
    edge[1] = jnp.where(live, hidden_of(east_parts), 0.0)

    load.wait()
    for j in range(2):
        for at, src in ((j, south), (rows + 2 + j, north)):
            left, right = side_rows(src[0, j], src[1, j], src[2, j])
            x_ref[at] = src[1, j].astype(bf16)
            xl_ref[at] = left.astype(bf16)
            xr_ref[at] = right.astype(bf16)
    for at in range(rows + 4, x_ref.shape[0]):
        for r in (x_ref, xl_ref, xr_ref):
            r[at] = jnp.zeros((32, 256), bf16)

    def shift_rows(i, _):
        t = i // 8
        wt, et = from_ref[0, t].astype(f32), from_ref[1, t].astype(f32)
        for k in range(8):
            y = i * 8 + k
            at = lax.rem(2 * y, 128)
            west = roll(wt, 127 - at)
            east = roll(et, 127 - at)
            left, right = put(x_ref[y + 2].astype(f32), west, east)
            xl_ref[y + 2] = left.astype(bf16)
            xr_ref[y + 2] = right.astype(bf16)
        return 0

    lax.fori_loop(0, rows // 8, shift_rows, 0)

    bias1 = jnp.concatenate([b1_ref[...]] * R1, axis=0)

    def hidden_rows(i, _):
        total = jnp.zeros((R1 * hid, 256), f32)
        for v, r in enumerate((xl_ref, x_ref, xr_ref)):
            piece = r[pl.ds(i * R1, R1 + 2)].reshape((R1 + 2) * 32, 256)
            total = total + jnp.dot(w1_ref[v], piece, preferred_element_type=f32)
        total = jnp.maximum(total + bias1, 0.0)
        h_ref[pl.ds(i * R1, R1)] = total.astype(bf16).reshape(R1, hid, 256)
        return 0

    lax.fori_loop(0, h_ref.shape[0] // R1, hidden_rows, 0)

    @pl.when(gy == 0)
    def _():
        h_ref[0] = jnp.zeros((hid, 256), bf16)

    @pl.when(is_top)
    def _():
        for k in range(3):
            q = fold_ref[lax.rem(gx + g_x - 1 + k, g_x)]
            qw, qe = lax.rem(q + g_x - 1, g_x), lax.rem(q + 1, g_x)
            parts = []
            for j in range(2):
                a, b, c = (top_ref[t, j].astype(f32) for t in (qw, q, qe))
                left, right = side_rows(a, b, c)
                parts += [left, b, right]
            a, b, c = (top_row(fold_ref[t]) for t in (qw, q, qe))
            left, right = side_rows(a, b, c)
            parts += [left, b, right]
            folded = mirror(hidden_of(parts).astype(bf16))
            if k == 1:
                h_ref[rows + 1] = folded.astype(bf16)
            else:
                tiles = rows // 64 + 1
                e = 0 if k == 0 else 1
                piece = roll(folded[:, 128:], 1) if k == 0 else folded[:, :128]
                edge[e, :, 128 * tiles :] = piece

    for e in range(2):
        h = edge[e]
        stack = jnp.concatenate([roll(h, -2 * (u - 1)).astype(bf16) for u in range(3)], axis=0)
        sums = jnp.dot(w2e_ref[e], stack, preferred_element_type=f32)
        for t in range(rows // 64 + 2):
            pedge[e, t] = sums[:, 128 * t : 128 * t + 128]

    outs = out_ref.shape[1]
    lane8 = lax.broadcasted_iota(jnp.int32, (outs, 256), 1)
    bias2 = b2_ref[...]

    def out_rows(i, _):
        piece = h_ref[pl.ds(i * R2, R2 + 2)].reshape((R2 + 2) * hid, 256)
        sums = jnp.dot(w2_ref[...], piece, preferred_element_type=f32)
        for k in range(R2):
            y = i * R2 + k
            t = y // 64 + 1
            at = lax.rem(2 * y, 128)
            a, b, c = (sums[(v * R2 + k) * outs : (v * R2 + k + 1) * outs] for v in range(3))
            west = roll(pedge[0, t], lax.rem(128 - at, 128))
            east = roll(pedge[1, t], 127 - at)
            a = jnp.where(lane8 == 0, jnp.concatenate([west, west], axis=1), roll(a, 1))
            c = jnp.where(lane8 == 255, jnp.concatenate([east, east], axis=1), roll(c, -1))
            m = jnp.broadcast_to(mask_ref[pl.ds(y, 1), :].astype(f32), (outs, 256))
            out_ref[y] = ((a + b + c + bias2) * m).astype(bf16)
        return 0

    lax.fori_loop(0, rows // R2, out_rows, 0)


def per_device(
    ocean_state, atm_blocks, dest_tile, dest_row, live_entry, land_mask, fold_pair, first_weight, first_bias,
    second_weight, second_bias,
):
    rows, levels4, cols = ocean_state.shape
    held, fields, block_cols = atm_blocks.shape
    g_y, g_x = lax.axis_size("gy"), lax.axis_size("gx")
    devices = g_y * g_x
    cap = max(2, 2 * held // devices)
    slots = devices * cap
    half = rows // 2
    cin = levels4 + fields
    hid, outs = first_weight.shape[2], second_weight.shape[2]
    tiles = rows // 64
    params = functools.partial(pltpu.CompilerParams, vmem_limit_bytes=60 * 2**20)

    outgoing, outgoing_rows = pl.pallas_call(
        functools.partial(pack_kernel, cap),
        out_shape=(jax.ShapeDtypeStruct((slots, fields, block_cols), bf16), jax.ShapeDtypeStruct((slots,), jnp.int32)),
        in_specs=[smem(), smem(), smem(), vmem()],
        out_specs=(vmem(), smem()),
        scratch_shapes=[pltpu.SMEM((devices,), jnp.int32)],
        name="pack",
    )(dest_tile.reshape(held), dest_row, live_entry, atm_blocks)
    incoming, incoming_rows = (
        lax.all_to_all(a, ("gy", "gx"), split_axis=0, concat_axis=0, tiled=True)
        for a in (outgoing.reshape(devices, cap, fields, block_cols), outgoing_rows.reshape(devices, cap))
    )
    spread = np.zeros((block_cols, cols), np.float32)
    spread[np.arange(cols) // 2, np.arange(cols)] = 1
    inputs, edge_cols = pl.pallas_call(
        combine_kernel,
        out_shape=(
            jax.ShapeDtypeStruct((rows, cin, cols), bf16),
            jax.ShapeDtypeStruct((2, tiles, cin, 128), bf16),
        ),
        in_specs=[smem()] + [vmem()] * 4,
        out_specs=(vmem(), vmem()),
        scratch_shapes=[pltpu.VMEM((half, fields, block_cols), f32), pltpu.VMEM((half, fields, cols), f32)],
        compiler_params=params(),
        name="combine",
    )(
        incoming_rows.reshape(slots), incoming.reshape(slots, fields, block_cols), ocean_state, land_mask,
        jnp.asarray(spread, bf16),
    )

    from_cols, rows_s, rows_n, top_all = pl.pallas_call(
        functools.partial(exchange_kernel, g_y, g_x),
        out_shape=(
            jax.ShapeDtypeStruct((2, tiles, cin, 128), bf16),
            jax.ShapeDtypeStruct((3, 2, cin, cols), bf16),
            jax.ShapeDtypeStruct((3, 2, cin, cols), bf16),
            jax.ShapeDtypeStruct((g_x, 2, cin, cols), bf16),
        ),
        in_specs=[anym(), anym()],
        out_specs=(anym(),) * 4,
        scratch_shapes=[
            pltpu.SemaphoreType.DMA((8 + g_x,)), pltpu.SemaphoreType.DMA((8 + g_x,)), pltpu.SemaphoreType.DMA,
        ],
        compiler_params=pltpu.CompilerParams(collective_id=0, has_side_effects=True),
        name="exchange",
    )(edge_cols, inputs)

    def band(r):
        t = np.zeros((3, r, r + 2), np.float32)
        for u in range(3):
            t[u, np.arange(r), np.arange(r) + u] = 1
        return jnp.asarray(t, bf16)

    w1 = jnp.einsum("urs,uvoc->vrosc", band(R1), first_weight).reshape(3, R1 * hid, (R1 + 2) * cin)
    w1s = first_weight.transpose(2, 0, 1, 3).reshape(hid, 9 * cin)
    w2 = jnp.einsum("urs,uvoc->vrosc", band(R2), second_weight).reshape(3 * R2 * outs, (R2 + 2) * hid)
    w2e = jnp.stack([second_weight[:, v].transpose(1, 0, 2).reshape(outs, 3 * hid) for v in (0, 2)])
    levels = levels4 // 4
    channel = np.arange(cin)
    negative = (channel < 2 * levels) | (channel == levels4) | (channel == levels4 + 1)
    signs = jnp.asarray(np.where(negative, -1.0, 1.0).astype(np.float32)[:, None])
    h_rows = -(-(rows + 2) // R1) * R1
    x_shape = (h_rows + 2, cin, cols)
    return pl.pallas_call(
        functools.partial(conv_kernel, g_y, g_x),
        out_shape=jax.ShapeDtypeStruct((rows, outs, cols), bf16),
        in_specs=[smem(), anym()] + [vmem()] * 13,
        out_specs=vmem(),
        scratch_shapes=[
            pltpu.VMEM(x_shape, bf16),
            pltpu.VMEM(x_shape, bf16),
            pltpu.VMEM(x_shape, bf16),
            pltpu.VMEM((h_rows, hid, cols), bf16),
            pltpu.VMEM((3, 2, cin, cols), f32),
            pltpu.VMEM((3, 2, cin, cols), f32),
            pltpu.VMEM((2, hid, 128 * (tiles + 2)), f32),
            pltpu.VMEM((2, tiles + 2, outs, 128), f32),
            pltpu.SemaphoreType.DMA,
        ],
        compiler_params=params(),
        name="conv",
    )(
        fold_pair, inputs, edge_cols, from_cols, rows_s, rows_n, top_all, land_mask, w1, w1s, first_bias[:, None], w2,
        w2e, second_bias[:, None], signs,
    )


def solution(mesh):
    return jax.shard_map(
        per_device,
        mesh=mesh,
        in_specs=(
            P("gy", None, "gx"),
            P(("gy", "gx"), None, None),
            P(("gy", "gx"), None),
            P(("gy", "gx")),
            P(("gy", "gx")),
            P("gy", "gx"),
            P(),
            P(),
            P(),
            P(),
            P(),
        ),
        out_specs=P("gy", None, "gx"),
        check_vma=False,
    )
```

time: 826 us -> 147 us (0.18); the launches traced: 811 us -> 147 us
  matrix products: 397 us -> 0.79 us
  local copies, waits for them, and re-layouts: 231 us -> 10.3 us
  Pallas kernels: 0 us -> 92.8 us
  other arithmetic: 82.3 us -> 1.28 us
  starting transfers between devices: 30.3 us -> 5.46 us
  blocking collectives: 29.6 us -> 11 us
  loops' own time: 14.3 us -> 0 us
    dot_general x217 -> x2, matrix products: 397 us -> 0.79 us  [the longest x1 0.51 us: per_device(): jnp.einsum('urs,uvoc->vrosc', band(R1), first_weight)]
    pallas_call x0 -> x4, Pallas kernels: none -> 92.8 us  [the longest x1 54.5 us: per_device(): pl.pallas_call(functools.partial(conv_kernel, g_y, g_x), out_shape=jax.Sh...]
    while x3 -> x0, local copies, waits for them, and re-layouts: 67.8 us -> none  [convolve(): lax.map(lambda number: block_out(number * row_block, row_block), jnp.aran...]
    concatenate x3 -> x0, other arithmetic: 50.5 us -> none  [with_halo(): shard = jnp.concatenate([before, shard, after], axis=dim)]
    scatter x3 -> x0, local copies, waits for them, and re-layouts: 47.7 us -> none  [the longest x1 25.1 us: per_device(): padded.at[tile_rows + 1]]
    concatenate x1 -> x0, local copies, waits for them, and re-layouts: 33 us -> none  [with_halo(): shard = jnp.concatenate([before, shard, after], axis=dim)]
    all_gather x2 -> x0, blocking collectives: 29.6 us -> none  [the longest x1 14.9 us: per_device(): gathered_hidden = lax.all_gather(top_hidden, 'gx', axis=1, tiled=True)]
    unnamed x16 -> x14, local copies, waits for them, and re-layouts: 26.4 us -> 0.03 us
  transfers between devices with their start and end apart: 10 -> 1, of which waited for: 3 -> 1; matrix products, arithmetic and copies ran while one was open for 10% -> 8% of each run, Pallas kernels for 0% -> 0%
where the time goes in v1:
time: 147 us
  Pallas kernels  92.8 us (63%)
  waiting for transfers between devices  25.2 us (17%)
  blocking collectives  11 us (7%)
  local copies, waits for them, and re-layouts  10.3 us (7%)
  starting transfers between devices  5.46 us (4%)
    pallas_call x1, Pallas kernels, per_device(): pl.pallas_call(functools.partial(conv_kernel, g_y, g_x), out_shape=jax.Sh...  54.5 us
    all_to_all x1, waiting for transfers between devices, per_device(): lax.all_to_all(a, ('gy', 'gx'), split_axis=0, concat_axis=0, tiled=True)  25.2 us
    pallas_call x1, Pallas kernels, per_device(): pl.pallas_call(combine_kernel, out_shape=(jax.ShapeDtypeStruct((rows, cin...  19.8 us
    pallas_call x1, Pallas kernels, per_device(): pl.pallas_call(functools.partial(exchange_kernel, g_y, g_x), out_shape=(j...  12 us
    all_to_all x1, blocking collectives, per_device(): lax.all_to_all(a, ('gy', 'gx'), split_axis=0, concat_axis=0, tiled=True)  11 us
    pallas_call x1, Pallas kernels, per_device(): pl.pallas_call(functools.partial(pack_kernel, cap), out_shape=(jax.ShapeD...  6.51 us
    all_to_all x1, starting transfers between devices, per_device(): lax.all_to_all(a, ('gy', 'gx'), split_axis=0, concat_axis=0, tiled=True)  5.46 us
    reshape x2, local copies, waits for them, and re-layouts, per_device(): jnp.einsum('urs,uvoc->vrosc', band(R1), first_weight)  4.01 us
  transfers between devices with their start and end apart: 1, of which 1 were waited for; matrix products, arithmetic and copies ran while one was open for 8% of the time, Pallas kernels for 0%

profile of v1, /device:TPU:6, one launch (start us, length us, event | category | flops | bytes accessed | tf_op | source)
XLA Modules:
  0.0 146.9 jit_solution(6065330108215610021)
XLA Ops:
  0.0 6.5 %pack.1 = (bf16[384,16,128]{2,1,0:T(8,128)(2,1)}, s32[384]{0:T(512)}) custom-call(s32[192]{0:T(256)} %bitcast.39, s32[192]{0:T(256)} %row_ref.1, s32[192]{0:T(256)} %live_ref.1, bf16[192,16,128]{2,1,0:T(8,128)(2,1)} %atm_ref.1), custom_call_target="tpu_custom_call" | custom-call | tf_op jit(solution)/shard_map/pack/pallas_call | solution.py:410
  6.5 0.8 all_to_all.9
  7.3 11.0 %all_to_all.14 = s32[32,1,12]{2,1,0:T(1,128)S(1)} all-to-all(s32[32,1,12]{2,1,0:T(1,128)S(1)} %bitcast.38), channel_id=1, replica_groups=mesh['gy'=4,'gx'=8] {'gy','gx'}, dimensions={0} | all-to-all | bytes 3072 | tf_op jit(solution)/shard_map/all_to_all | solution.py:419
  18.3 0.0 copy-start.2
  18.3 5.5 %all-to-all-start.1 = ((bf16[32,12,16,128]{3,2,1,0:T(8,128)(2,1)}), bf16[32,12,16,128]{3,2,1,0:T(8,128)(2,1)}, u32[]{:S(2)}, u32[]{:S(2)}) async-start(bf16[32,12,16,128]{3,2,1,0:T(8,128)(2,1)} %bitcast.36), calls=%async_computation.1 | async-start | bytes 3145728 | tf_op jit(solution)/shard_map/all_to_all | solution.py:419
  23.7 0.7 copy.45.b2_ref
  24.4 0.0 copy-done.1
  24.4 0.7 stack_reshape.6
  25.1 0.7 stack_reshape.7
  25.8 0.7 copy.44.b1_ref
  26.5 0.7 copy.43.w1s_ref
  27.2 0.3 convolution_bitcast_fusion.1
  27.5 0.9 reshape.32.w2_ref
  28.4 0.5 convolution_bitcast_fusion
  28.9 1.6 %copy.47 = bf16[3,6,64,8,32]{4,3,2,1,0:T(8,128)(2,1)S(1)} copy(bf16[3,6,64,8,32]{2,3,4,0,1:T(8,128)(2,1)S(1)} %convolution_bitcast_fusion) | data formatting | bytes 1179648 | tf_op jit(solution)/shard_map/reshape | solution.py:463
  30.6 2.4 %reshape.36.w1_ref = bf16[3,384,256]{2,1,0:T(8,128)(2,1)} reshape(bf16[3,6,64,8,32]{4,3,2,1,0:T(8,128)(2,1)S(1)} %copy.47) | data formatting | bytes 1179648 | tf_op jit(solution)/shard_map/reshape | solution.py:463
  33.0 0.6 pad_maximum_fusion.w2e_ref
  33.6 0.5 broadcast.3
  34.1 0.7 reduce.3
  34.8 0.6 reshape.27.rows_ref
  35.4 25.2 %all-to-all-done.1 = bf16[32,12,16,128]{3,2,1,0:T(8,128)(2,1)} async-done(((bf16[32,12,16,128]{3,2,1,0:T(8,128)(2,1)}), bf16[32,12,16,128]{3,2,1,0:T(8,128)(2,1)}, u32[]{:S(2)}, u32[]{:S(2)}) %all-to-all-start.1) | async-done | bytes 1572896 | tf_op jit(solution)/shard_map/all_to_all | solution.py:419
  60.6 19.8 %combine.1 = (bf16[384,32,256]{2,1,0:T(8,128)(2,1)}, bf16[2,6,32,128]{3,2,1,0:T(8,128)(2,1)}) custom-call(s32[384]{0:T(512)} %reshape.27.rows_ref, bf16[384,16,128]{2,1,0:T(8,128)(2,1)} %bitcast.3.blocks_ref, bf16[384,16,256]{2,1,0:T(8,128)(2,1)} %state_ref.1, s32[384,256]{1,0:T(8,128)} %mask_ref.3, bf16[128,256]{1,0:T(8,128)(2,1)} %constant.6.clone.up_ref), custom_call_target="tpu_custom_call" | custom-call | tf_op jit(solution)/shard_map/combine/pallas_call | solution.py:424
  80.4 12.0 %exchange.1 = (bf16[2,6,32,128]{3,2,1,0:T(8,128)(2,1)}, bf16[3,2,32,256]{3,2,1,0:T(8,128)(2,1)}, bf16[3,2,32,256]{3,2,1,0:T(8,128)(2,1)}, bf16[8,2,32,256]{3,2,1,0:T(8,128)(2,1)}) custom-call(bf16[2,6,32,128]{3,2,1,0:T(8,128)(2,1)} %get-tuple-element.16.cols_ref, bf16[384,32,256]{2,1,0:T(8,128)(2,1)} %get-tuple-element.15.inp_ref), custom_call_target="tpu_custom_call" | custom-call | tf_op jit(solution)/shard_map/exchange/pallas_call | solution.py:440
  92.4 54.5 %conv.1 = bf16[384,8,256]{2,1,0:T(8,128)(2,1)} custom-call(s32[8]{0:T(128)} %fold_ref.1, bf16[384,32,256]{2,1,0:T(8,128)(2,1)} %get-tuple-element.15.inp_ref, bf16[2,6,32,128]{3,2,1,0:T(8,128)(2,1)} %get-tuple-element.16.cols_ref, bf16[2,6,32,128]{3,2,1,0:T(8,128)(2,1)} %get-tuple-element.17.from_ref, bf16[3,2,32,256]{3,2,1,0:T(8,128)(2,1)} %get-tuple-element.18.rs_ref, ...), custom_call_target="tpu_custom_call" | custom-call | tf_op jit(solution)/shard_map/conv/pallas_call | solution.py:473
  (16 shorter events, 0.1 us)
Async XLA Ops:
  18.2 5.5 %copy-start.6 = (f32[8]{0:T(128)S(1)}, f32[8]{0:T(128)}, u32[]{:S(2)}) copy-start(f32[8]{0:T(128)} %param.25) | copy-start | bytes 100
  18.2 6.2 %copy-start.1 = (bf16[3,3,8,64]{3,2,1,0:T(8,128)(2,1)S(1)}, bf16[3,3,8,64]{3,2,1,0:T(8,128)(2,1)}, u32[]{:S(2)}) copy-start(bf16[3,3,8,64]{3,2,1,0:T(8,128)(2,1)} %param.24) | copy-start | bytes 27652
  18.2 7.5 %copy-start.5 = (f32[64]{0:T(128)S(1)}, f32[64]{0:T(128)}, u32[]{:S(2)}) copy-start(f32[64]{0:T(128)} %param.23) | copy-start | bytes 772
  18.2 8.2 %copy-start = (bf16[3,3,64,32]{2,3,1,0:T(8,128)(2,1)S(1)}, bf16[3,3,64,32]{2,3,1,0:T(8,128)(2,1)}, u32[]{:S(2)}) copy-start(bf16[3,3,64,32]{2,3,1,0:T(8,128)(2,1)} %param.22) | copy-start | bytes 110596
  18.3 9.0 %copy-start.2 = (bf16[3,6,8,1,1]{2,0,4,3,1:T(4,128)(2,1)S(1)}, bf16[3,6,8,1,1]{2,0,4,3,1:T(4,128)(2,1)}, u32[]{:S(2)}) copy-start(bf16[3,6,8,1,1]{2,0,4,3,1:T(4,128)(2,1)} %constant.9) | copy-start | bytes 868
  18.3 42.4 %all-to-all-start.1 = ((bf16[32,12,16,128]{3,2,1,0:T(8,128)(2,1)}), bf16[32,12,16,128]{3,2,1,0:T(8,128)(2,1)}, u32[]{:S(2)}, u32[]{:S(2)}) async-start(bf16[32,12,16,128]{3,2,1,0:T(8,128)(2,1)} %bitcast.36), calls=%async_computation.1 | async-start | bytes 3145728 | tf_op jit(solution)/shard_map/all_to_all | solution.py:419
  30.6 2.4 %copy-start.3 = (bf16[1,8,192]{2,1,0:T(8,128)(2,1)S(1)}, bf16[1,8,192]{2,1,0:T(8,128)(2,1)}, u32[]{:S(2)}) copy-start(bf16[1,8,192]{2,1,0:T(8,128)(2,1)} %stack_reshape.6) | copy-start | bytes 9220
  30.6 2.4 %copy-start.4 = (bf16[1,8,192]{2,1,0:T(8,128)(2,1)S(1)}, bf16[1,8,192]{2,1,0:T(8,128)(2,1)}, u32[]{:S(2)}) copy-start(bf16[1,8,192]{2,1,0:T(8,128)(2,1)} %stack_reshape.7) | copy-start | bytes 9220

commit v2 on v1

--- a/solution.py
+++ b/solution.py
@@ -11,6 +11,7 @@
 MESH = pl.DeviceIdType.MESH
 R1 = 6
 R2 = 6
+GROUP = 5
 f32 = jnp.float32
 bf16 = jnp.bfloat16
 
@@ -27,50 +28,47 @@
     return pl.BlockSpec(memory_space=pl.ANY)
 
 
-def pack_kernel(cap, tile_ref, row_ref, live_ref, atm_ref, out_ref, rows_ref, count):
-    devices = count.shape[0]
+def pack_kernel(tile_ref, row_ref, live_ref, atm_ref, out_ref, count, names, *, empty):
+    devices, cap = out_ref.shape[0], out_ref.shape[1] - 1
+    names[...] = jnp.full(names.shape, empty, f32)
+    lane = lax.broadcasted_iota(jnp.int32, (8, 128), 1)
 
     def clear(i, _):
         count[i] = 0
         return 0
 
-    def clear_rows(i, _):
-        rows_ref[i] = -1
-        return 0
-
-    lax.fori_loop(0, devices, clear, 0)
-    lax.fori_loop(0, rows_ref.shape[0], clear_rows, 0, unroll=8)
+    lax.fori_loop(0, devices, clear, 0, unroll=8)
 
     def place(e, _):
-        @pl.when(live_ref[e] == 1)
-        def _():
-            t = tile_ref[e]
-            c = count[t]
-            count[t] = c + 1
-            slot = t * cap + c
-            rows_ref[slot] = row_ref[e]
-            out_ref[slot] = atm_ref[e]
-
-        return 0
-
-    lax.fori_loop(0, atm_ref.shape[0], place, 0)
+        t, live = tile_ref[e], live_ref[e]
+        c = count[t]
+        count[t] = c + live
+        out_ref[t, jnp.where(live == 1, c, cap)] = atm_ref[e]
+        names[t] = jnp.where(lane == jnp.where(live == 1, c, -1), row_ref[e].astype(f32), names[t])
+        return 0
+
+    lax.fori_loop(0, atm_ref.shape[0], place, 0, unroll=8)
+
+    def name(t, _):
+        out_ref[t, cap] = jnp.concatenate([names[t], names[t]], axis=0).astype(bf16)
+        return 0
+
+    lax.fori_loop(0, devices, name, 0, unroll=4)
 
 
 def combine_kernel(rows_ref, blocks_ref, state_ref, mask_ref, up_ref, inp_ref, cols_ref, acc, up):
-    half = acc.shape[0]
+    half = acc.shape[0] - 1
+    slots = blocks_ref.shape[1] - 1
     tile_rows, levels = state_ref.shape[0], state_ref.shape[1]
     acc[...] = jnp.zeros_like(acc)
 
-    def add(s, _):
-        r = rows_ref[s]
-
-        @pl.when(r >= 0)
-        def _():
-            acc[r] += blocks_ref[s].astype(f32)
-
-        return 0
-
-    lax.fori_loop(0, rows_ref.shape[0], add, 0, unroll=4)
+    def add(d, _):
+        for k in range(slots):
+            r = rows_ref[d * slots + k]
+            acc[r] += blocks_ref[d, k].astype(f32)
+        return 0
+
+    lax.fori_loop(0, blocks_ref.shape[0], add, 0)
 
     def spread(i, _):
         piece = acc[pl.ds(i * 8, 8)].astype(bf16).reshape(8 * 16, 128)
@@ -220,7 +218,7 @@
 
 def conv_kernel(
     g_y, g_x, fold_ref, inp_ref, cols_ref, from_ref, rs_ref, rn_ref, top_ref, mask_ref, w1_ref, w1s_ref, b1_ref, w2_ref,
-    w2e_ref, b2_ref, sign_ref, out_ref, x_ref, xl_ref, xr_ref, h_ref, north, south, edge, pedge, sem,
+    w2e_ref, b2_ref, sign_ref, out_ref, x_ref, far_ref, h_ref, north, south, edge, pedge, sem,
 ):
     gy, gx = lax.axis_index("gy"), lax.axis_index("gx")
     rows = out_ref.shape[0]
@@ -286,6 +284,9 @@
         total = jnp.dot(w1s_ref[...], stack, preferred_element_type=f32)
         return jnp.maximum(total + b1_ref[...], 0.0)
 
+    for t in range(rows // 64 + 2):
+        far_ref[0, t] = far_w[:, 128 * t : 128 * t + 128]
+        far_ref[1, t] = far_e[:, 128 * t : 128 * t + 128]
     west_parts, east_parts = [], []
     for u in range(3):
         s = -2 * (u - 1)
@@ -298,42 +299,31 @@
 
     load.wait()
     for j in range(2):
-        for at, src in ((j, south), (rows + 2 + j, north)):
-            left, right = side_rows(src[0, j], src[1, j], src[2, j])
-            x_ref[at] = src[1, j].astype(bf16)
-            xl_ref[at] = left.astype(bf16)
-            xr_ref[at] = right.astype(bf16)
+        x_ref[j] = south[1, j].astype(bf16)
+        x_ref[rows + 2 + j] = north[1, j].astype(bf16)
     for at in range(rows + 4, x_ref.shape[0]):
-        for r in (x_ref, xl_ref, xr_ref):
-            r[at] = jnp.zeros((32, 256), bf16)
-
-    def shift_rows(i, _):
-        t = i // 8
-        wt, et = from_ref[0, t].astype(f32), from_ref[1, t].astype(f32)
-        for k in range(8):
-            y = i * 8 + k
-            at = lax.rem(2 * y, 128)
-            west = roll(wt, 127 - at)
-            east = roll(et, 127 - at)
-            left, right = put(x_ref[y + 2].astype(f32), west, east)
-            xl_ref[y + 2] = left.astype(bf16)
-            xr_ref[y + 2] = right.astype(bf16)
-        return 0
-
-    lax.fori_loop(0, rows // 8, shift_rows, 0)
+        x_ref[at] = jnp.zeros((32, 256), bf16)
 
     bias1 = jnp.concatenate([b1_ref[...]] * R1, axis=0)
+    weights = jnp.concatenate([w1_ref[v] for v in range(3)], axis=1)
 
     def hidden_rows(i, _):
-        total = jnp.zeros((R1 * hid, 256), f32)
-        for v, r in enumerate((xl_ref, x_ref, xr_ref)):
-            piece = r[pl.ds(i * R1, R1 + 2)].reshape((R1 + 2) * 32, 256)
-            total = total + jnp.dot(w1_ref[v], piece, preferred_element_type=f32)
-        total = jnp.maximum(total + bias1, 0.0)
-        h_ref[pl.ds(i * R1, R1)] = total.astype(bf16).reshape(R1, hid, 256)
-        return 0
-
-    lax.fori_loop(0, h_ref.shape[0] // R1, hidden_rows, 0)
+        first = i * (GROUP * R1)
+        shifted = []
+        for k in range(GROUP * R1 + 2):
+            at = 124 + 2 * (first + k)
+            t, lane = at // 128, lax.rem(at, 128)
+            x = x_ref[first + k]
+            left, right = put(x.astype(f32), roll(far_ref[0, t], 127 - lane), roll(far_ref[1, t], 127 - lane))
+            shifted.append((left.astype(bf16), x, right.astype(bf16)))
+        for b in range(GROUP):
+            piece = jnp.concatenate([row[v] for v in range(3) for row in shifted[b * R1 : b * R1 + R1 + 2]], axis=0)
+            total = jnp.dot(weights, piece, preferred_element_type=f32)
+            total = jnp.maximum(total + bias1, 0.0)
+            h_ref[pl.ds(first + b * R1, R1)] = total.astype(bf16).reshape(R1, hid, 256)
+        return 0
+
+    lax.fori_loop(0, h_ref.shape[0] // (GROUP * R1), hidden_rows, 0)
 
     @pl.when(gy == 0)
     def _():
@@ -388,7 +378,7 @@
             out_ref[y] = ((a + b + c + bias2) * m).astype(bf16)
         return 0
 
-    lax.fori_loop(0, rows // R2, out_rows, 0)
+    lax.fori_loop(0, rows // R2, out_rows, 0, unroll=4)
 
 
 def per_device(
@@ -407,18 +397,17 @@
     tiles = rows // 64
     params = functools.partial(pltpu.CompilerParams, vmem_limit_bytes=60 * 2**20)
 
-    outgoing, outgoing_rows = pl.pallas_call(
-        functools.partial(pack_kernel, cap),
-        out_shape=(jax.ShapeDtypeStruct((slots, fields, block_cols), bf16), jax.ShapeDtypeStruct((slots,), jnp.int32)),
+    assert half <= 256 and cap <= 128
+    outgoing = pl.pallas_call(
+        functools.partial(pack_kernel, empty=half),
+        out_shape=jax.ShapeDtypeStruct((devices, cap + 1, fields, block_cols), bf16),
         in_specs=[smem(), smem(), smem(), vmem()],
-        out_specs=(vmem(), smem()),
-        scratch_shapes=[pltpu.SMEM((devices,), jnp.int32)],
+        out_specs=vmem(),
+        scratch_shapes=[pltpu.SMEM((devices,), jnp.int32), pltpu.VMEM((devices, 8, 128), f32)],
         name="pack",
     )(dest_tile.reshape(held), dest_row, live_entry, atm_blocks)
-    incoming, incoming_rows = (
-        lax.all_to_all(a, ("gy", "gx"), split_axis=0, concat_axis=0, tiled=True)
-        for a in (outgoing.reshape(devices, cap, fields, block_cols), outgoing_rows.reshape(devices, cap))
-    )
+    incoming = lax.all_to_all(outgoing, ("gy", "gx"), split_axis=0, concat_axis=0, tiled=True)
+    incoming_rows = incoming[:, cap, 0, :cap].astype(jnp.int32)
     spread = np.zeros((block_cols, cols), np.float32)
     spread[np.arange(cols) // 2, np.arange(cols)] = 1
     inputs, edge_cols = pl.pallas_call(
@@ -429,11 +418,11 @@
         ),
         in_specs=[smem()] + [vmem()] * 4,
         out_specs=(vmem(), vmem()),
-        scratch_shapes=[pltpu.VMEM((half, fields, block_cols), f32), pltpu.VMEM((half, fields, cols), f32)],
+        scratch_shapes=[pltpu.VMEM((half + 1, fields, block_cols), f32), pltpu.VMEM((half, fields, cols), f32)],
         compiler_params=params(),
         name="combine",
     )(
-        incoming_rows.reshape(slots), incoming.reshape(slots, fields, block_cols), ocean_state, land_mask,
+        incoming_rows.reshape(slots), incoming, ocean_state, land_mask,
         jnp.asarray(spread, bf16),
     )
 
@@ -468,7 +457,7 @@
     channel = np.arange(cin)
     negative = (channel < 2 * levels) | (channel == levels4) | (channel == levels4 + 1)
     signs = jnp.asarray(np.where(negative, -1.0, 1.0).astype(np.float32)[:, None])
-    h_rows = -(-(rows + 2) // R1) * R1
+    h_rows = -(-(rows + 2) // (GROUP * R1)) * (GROUP * R1)
     x_shape = (h_rows + 2, cin, cols)
     return pl.pallas_call(
         functools.partial(conv_kernel, g_y, g_x),
@@ -477,8 +466,7 @@
         out_specs=vmem(),
         scratch_shapes=[
             pltpu.VMEM(x_shape, bf16),
-            pltpu.VMEM(x_shape, bf16),
-            pltpu.VMEM(x_shape, bf16),
+            pltpu.VMEM((2, tiles + 2, cin, 128), f32),
             pltpu.VMEM((h_rows, hid, cols), bf16),
             pltpu.VMEM((3, 2, cin, cols), f32),
             pltpu.VMEM((3, 2, cin, cols), f32),

time: 147 us -> 109 us (0.74)
  Pallas kernels: 92.8 us -> 61.3 us
  blocking collectives: 11 us -> 0 us
  waiting for transfers between devices: 25.2 us -> 31 us
  local copies, waits for them, and re-layouts: 10.3 us -> 7.9 us
    pallas_call x1, Pallas kernels: 54.5 us -> 28 us  [per_device(): pl.pallas_call(functools.partial(conv_kernel, g_y, g_x), out_shape=jax.Sh...]
    all_to_all x1 -> x0, blocking collectives: 11 us -> none  [per_device(): lax.all_to_all(a, ('gy', 'gx'), split_axis=0, concat_axis=0, tiled=True)]
    all_to_all x1, waiting for transfers between devices: 25.2 us -> 31 us  [per_device(): lax.all_to_all(outgoing, ('gy', 'gx'), split_axis=0, concat_axis=0, tiled...]
    pallas_call x1, Pallas kernels: 6.51 us -> 3.55 us  [per_device(): pl.pallas_call(functools.partial(pack_kernel, empty=half), out_shape=jax....]
    pallas_call x1, Pallas kernels: 19.8 us -> 17.8 us  [per_device(): pl.pallas_call(combine_kernel, out_shape=(jax.ShapeDtypeStruct((rows, cin...]
where the time goes in v2:
time: 109 us
  Pallas kernels  61.3 us (56%)
  waiting for transfers between devices  31 us (28%)
  local copies, waits for them, and re-layouts  7.9 us (7%)
  starting transfers between devices  6.13 us (6%)
  other arithmetic  1.5 us (1%)
    all_to_all x1, waiting for transfers between devices, per_device(): lax.all_to_all(outgoing, ('gy', 'gx'), split_axis=0, concat_axis=0, tiled...  31 us
    pallas_call x1, Pallas kernels, per_device(): pl.pallas_call(functools.partial(conv_kernel, g_y, g_x), out_shape=jax.Sh...  28 us
    pallas_call x1, Pallas kernels, per_device(): pl.pallas_call(combine_kernel, out_shape=(jax.ShapeDtypeStruct((rows, cin...  17.8 us
    pallas_call x1, Pallas kernels, per_device(): pl.pallas_call(functools.partial(exchange_kernel, g_y, g_x), out_shape=(j...  12.1 us
    all_to_all x1, starting transfers between devices, per_device(): lax.all_to_all(outgoing, ('gy', 'gx'), split_axis=0, concat_axis=0, tiled...  6.13 us
    reshape x2, local copies, waits for them, and re-layouts, per_device(): jnp.einsum('urs,uvoc->vrosc', band(R1), first_weight)  4.01 us
    pallas_call x1, Pallas kernels, per_device(): pl.pallas_call(functools.partial(pack_kernel, empty=half), out_shape=jax....  3.55 us
  transfers between devices with their start and end apart: 1, of which 1 were waited for; matrix products, arithmetic and copies ran while one was open for 8% of the time, Pallas kernels for 0%

profile of v2, /device:TPU:6, one launch (start us, length us, event | category | flops | bytes accessed | tf_op | source)
XLA Modules:
  0.0 108.7 jit_solution(12376873336248045273)
XLA Ops:
  0.0 3.5 %pack.1 = bf16[32,13,16,128]{3,2,1,0:T(8,128)(2,1)} custom-call(s32[192]{0:T(256)} %bitcast.34, s32[192]{0:T(256)} %row_ref.1, s32[192]{0:T(256)} %live_ref.1, bf16[192,16,128]{2,1,0:T(8,128)(2,1)} %atm_ref.1), custom_call_target="tpu_custom_call" | custom-call | tf_op jit(solution)/shard_map/pack/pallas_call | solution.py:401
  3.6 0.0 copy-start.2
  3.6 6.1 %all-to-all-start = ((bf16[32,13,16,128]{3,2,1,0:T(8,128)(2,1)}), bf16[32,13,16,128]{3,2,1,0:T(8,128)(2,1)}, u32[]{:S(2)}, u32[]{:S(2)}) async-start(bf16[32,13,16,128]{3,2,1,0:T(8,128)(2,1)} %pack.1), calls=%async_computation | async-start | bytes 3407872 | tf_op jit(solution)/shard_map/all_to_all | solution.py:409
  9.7 0.0 copy-done.4
  9.7 0.7 copy.34.b2_ref
  10.4 0.0 copy-done.1
  10.4 0.1 stack_reshape.6
  10.5 0.1 stack_reshape.7
  10.6 0.0 copy-done.3
  10.6 0.7 copy.33.b1_ref
  11.3 0.0 copy-done
  11.3 0.7 copy.32.w1s_ref
  12.0 0.3 convolution_bitcast_fusion.1
  12.3 0.9 reshape.19.w2_ref
  13.2 0.5 convolution_bitcast_fusion
  13.7 1.6 %copy.36 = bf16[3,6,64,8,32]{4,3,2,1,0:T(8,128)(2,1)S(1)} copy(bf16[3,6,64,8,32]{2,3,4,0,1:T(8,128)(2,1)S(1)} %convolution_bitcast_fusion) | data formatting | bytes 1179648 | tf_op jit(solution)/shard_map/reshape | solution.py:452
  15.3 2.4 %reshape.24.w1_ref = bf16[3,384,256]{2,1,0:T(8,128)(2,1)} reshape(bf16[3,6,64,8,32]{4,3,2,1,0:T(8,128)(2,1)S(1)} %copy.36) | data formatting | bytes 1179648 | tf_op jit(solution)/shard_map/reshape | solution.py:452
  17.7 0.6 pad_maximum_fusion.w2e_ref
  18.3 31.0 %all-to-all-done.blocks_ref = bf16[32,13,16,128]{3,2,1,0:T(8,128)(2,1)} async-done(((bf16[32,13,16,128]{3,2,1,0:T(8,128)(2,1)}), bf16[32,13,16,128]{3,2,1,0:T(8,128)(2,1)}, u32[]{:S(2)}, u32[]{:S(2)}) %all-to-all-start) | async-done | bytes 1703968 | tf_op jit(solution)/shard_map/all_to_all | solution.py:409
  49.3 0.9 fusion.4
  50.2 0.7 reshape.20.rows_ref
  50.9 17.8 %combine.1 = (bf16[384,32,256]{2,1,0:T(8,128)(2,1)}, bf16[2,6,32,128]{3,2,1,0:T(8,128)(2,1)}) custom-call(s32[384]{0:T(512)} %reshape.20.rows_ref, bf16[32,13,16,128]{3,2,1,0:T(8,128)(2,1)} %all-to-all-done.blocks_ref, bf16[384,16,256]{2,1,0:T(8,128)(2,1)} %state_ref.1, s32[384,256]{1,0:T(8,128)} %mask_ref.3, bf16[128,256]{1,0:T(8,128)(2,1)} %constant.6.clone.up_ref), custom_call_target="tpu_custom_call" | custom-call | tf_op jit(solution)/shard_map/combine/pallas_call | solution.py:413
  68.7 12.1 %exchange.1 = (bf16[2,6,32,128]{3,2,1,0:T(8,128)(2,1)}, bf16[3,2,32,256]{3,2,1,0:T(8,128)(2,1)}, bf16[3,2,32,256]{3,2,1,0:T(8,128)(2,1)}, bf16[8,2,32,256]{3,2,1,0:T(8,128)(2,1)}) custom-call(bf16[2,6,32,128]{3,2,1,0:T(8,128)(2,1)} %get-tuple-element.12.cols_ref, bf16[384,32,256]{2,1,0:T(8,128)(2,1)} %get-tuple-element.11.inp_ref), custom_call_target="tpu_custom_call" | custom-call | tf_op jit(solution)/shard_map/exchange/pallas_call | solution.py:429
  80.7 28.0 %conv.1 = bf16[384,8,256]{2,1,0:T(8,128)(2,1)} custom-call(s32[8]{0:T(128)} %fold_ref.1, bf16[384,32,256]{2,1,0:T(8,128)(2,1)} %get-tuple-element.11.inp_ref, bf16[2,6,32,128]{3,2,1,0:T(8,128)(2,1)} %get-tuple-element.12.cols_ref, bf16[2,6,32,128]{3,2,1,0:T(8,128)(2,1)} %get-tuple-element.13.from_ref, bf16[3,2,32,256]{3,2,1,0:T(8,128)(2,1)} %get-tuple-element.14.rs_ref, ...), custom_call_target="tpu_custom_call" | custom-call | tf_op jit(solution)/shard_map/conv/pallas_call | solution.py:462
  (9 shorter events, 0.0 us)
Async XLA Ops:
  3.5 6.2 %copy-start.4 = (f32[8]{0:T(128)S(1)}, f32[8]{0:T(128)}, u32[]{:S(2)}) copy-start(f32[8]{0:T(128)} %param.25) | copy-start | bytes 100
  3.5 6.8 %copy-start.1 = (bf16[3,3,8,64]{3,2,1,0:T(8,128)(2,1)S(1)}, bf16[3,3,8,64]{3,2,1,0:T(8,128)(2,1)}, u32[]{:S(2)}) copy-start(bf16[3,3,8,64]{3,2,1,0:T(8,128)(2,1)} %param.24) | copy-start | bytes 27652
  3.6 7.0 %copy-start.3 = (f32[64]{0:T(128)S(1)}, f32[64]{0:T(128)}, u32[]{:S(2)}) copy-start(f32[64]{0:T(128)} %param.23) | copy-start | bytes 772
  3.6 7.7 %copy-start = (bf16[3,3,64,32]{2,3,1,0:T(8,128)(2,1)S(1)}, bf16[3,3,64,32]{2,3,1,0:T(8,128)(2,1)}, u32[]{:S(2)}) copy-start(bf16[3,3,64,32]{2,3,1,0:T(8,128)(2,1)} %param.22) | copy-start | bytes 110596
  3.6 8.4 %copy-start.2 = (bf16[3,6,8,1,1]{2,0,4,3,1:T(4,128)(2,1)S(1)}, bf16[3,6,8,1,1]{2,0,4,3,1:T(4,128)(2,1)}, u32[]{:S(2)}) copy-start(bf16[3,6,8,1,1]{2,0,4,3,1:T(4,128)(2,1)} %constant.9) | copy-start | bytes 868
  3.6 45.7 %all-to-all-start = ((bf16[32,13,16,128]{3,2,1,0:T(8,128)(2,1)}), bf16[32,13,16,128]{3,2,1,0:T(8,128)(2,1)}, u32[]{:S(2)}, u32[]{:S(2)}) async-start(bf16[32,13,16,128]{3,2,1,0:T(8,128)(2,1)} %pack.1), calls=%async_computation | async-start | bytes 3407872 | tf_op jit(solution)/shard_map/all_to_all | solution.py:409

commit v3 on v2

--- a/solution.py
+++ b/solution.py
@@ -56,62 +56,82 @@
     lax.fori_loop(0, devices, name, 0, unroll=4)
 
 
-def combine_kernel(rows_ref, blocks_ref, state_ref, mask_ref, up_ref, inp_ref, cols_ref, acc, up):
-    half = acc.shape[0] - 1
-    slots = blocks_ref.shape[1] - 1
-    tile_rows, levels = state_ref.shape[0], state_ref.shape[1]
-    acc[...] = jnp.zeros_like(acc)
-
-    def add(d, _):
-        for k in range(slots):
-            r = rows_ref[d * slots + k]
-            acc[r] += blocks_ref[d, k].astype(f32)
-        return 0
-
-    lax.fori_loop(0, blocks_ref.shape[0], add, 0)
-
-    def spread(i, _):
-        piece = acc[pl.ds(i * 8, 8)].astype(bf16).reshape(8 * 16, 128)
-        wide = jnp.dot(piece, up_ref[...], preferred_element_type=f32)
-        up[pl.ds(i * 8, 8)] = wide.reshape(8, 16, 256)
-        return 0
-
-    lax.fori_loop(0, half // 8, spread, 0)
-
-    lane = lax.broadcasted_iota(jnp.int32, (32, 128), 1)
+def mask_rows(mask_ref, out_ref, values, done):
+    rows, count, cols = out_ref.shape
+    lane = lax.broadcasted_iota(jnp.int32, (count, 128), 1)
 
     def rows8(i, carry):
         lo, hi = carry
         m = mask_ref[pl.ds(i * 8, 8), :].astype(f32)
         for k in range(8):
             y = i * 8 + k
-            mk = jnp.broadcast_to(m[k : k + 1, :], (16, 256))
-            a = state_ref[y].astype(f32) * mk
-            b = up[i * 4 + k // 2] * mk
-            full = jnp.concatenate([a, b], axis=0)
-            inp_ref[y] = full.astype(bf16)
+            full = values(i, k) * jnp.broadcast_to(m[k : k + 1, :], (count, cols))
+            out_ref[y] = full.astype(bf16)
             at = lax.rem(2 * y, 128)
             here = (lane >> 1) == lax.rem(y, 64)
             lo = jnp.where(here, pltpu.roll(full[:, :128], at, 1), lo)
             hi = jnp.where(here, pltpu.roll(full[:, 128:], lax.rem(at + 2, 128), 1), hi)
         return lo, hi
 
-    zero = jnp.zeros((32, 128), f32)
+    zero = jnp.zeros((count, 128), f32)
 
     def tile(t, _):
         lo, hi = lax.fori_loop(t * 8, t * 8 + 8, rows8, (zero, zero))
-        cols_ref[0, t] = lo.astype(bf16)
-        cols_ref[1, t] = hi.astype(bf16)
-        return 0
-
-    lax.fori_loop(0, tile_rows // 64, tile, 0)
-
-
-def exchange_kernel(g_y, g_x, cols_ref, inp_ref, from_cols, rows_s, rows_n, top_all, send, recv, own):
+        done(t, lo.astype(bf16), hi.astype(bf16))
+        return 0
+
+    lax.fori_loop(0, rows // 64, tile, 0)
+
+
+def state_kernel(state_ref, mask_ref, out_ref, cols_ref, ends_ref):
+    rows = out_ref.shape[0]
+
+    def done(t, lo, hi):
+        cols_ref[0, t] = lo
+        cols_ref[1, t] = hi
+
+    mask_rows(mask_ref, out_ref, lambda i, k: state_ref[i * 8 + k].astype(f32), done)
+    for j in range(2):
+        ends_ref[0, j] = out_ref[j]
+        ends_ref[1, j] = out_ref[rows - 2 + j]
+
+
+def forcing_kernel(rows_ref, blocks_ref, mask_ref, up_ref, cs_ref, es_ref, out_ref, cols_ref, ends_ref, acc, up):
+    half = acc.shape[0] - 1
+    slots = blocks_ref.shape[1] - 1
+    rows = out_ref.shape[0]
+    acc[...] = jnp.zeros_like(acc)
+
+    def add(d, _):
+        for k in range(slots):
+            r = rows_ref[d * slots + k]
+            acc[r] += blocks_ref[d, k].astype(f32)
+        return 0
+
+    lax.fori_loop(0, blocks_ref.shape[0], add, 0)
+
+    def spread(i, _):
+        piece = acc[pl.ds(i * 16, 16)].astype(bf16).reshape(16 * 16, 128)
+        wide = jnp.dot(piece, up_ref[...], preferred_element_type=f32)
+        up[pl.ds(i * 16, 16)] = wide.reshape(16, 16, 256)
+        return 0
+
+    lax.fori_loop(0, half // 16, spread, 0, unroll=4)
+
+    def done(t, lo, hi):
+        cols_ref[0, t] = jnp.concatenate([cs_ref[0, t], lo], axis=0)
+        cols_ref[1, t] = jnp.concatenate([cs_ref[1, t], hi], axis=0)
+
+    mask_rows(mask_ref, out_ref, lambda i, k: up[i * 4 + k // 2], done)
+    for j in range(2):
+        ends_ref[0, j] = jnp.concatenate([es_ref[0, j], out_ref[j]], axis=0)
+        ends_ref[1, j] = jnp.concatenate([es_ref[1, j], out_ref[rows - 2 + j]], axis=0)
+
+
+def exchange_kernel(g_y, g_x, cols_ref, ends_ref, from_cols, rows_s, rows_n, top_all, send, recv, own):
     gy, gx = lax.axis_index("gy"), lax.axis_index("gx")
-    n_rows = inp_ref.shape[0]
     west, east = lax.rem(gx + g_x - 1, g_x), lax.rem(gx + 1, g_x)
-    low, high = inp_ref.at[pl.ds(0, 2)], inp_ref.at[pl.ds(n_rows - 2, 2)]
+    low, high = ends_ref.at[0], ends_ref.at[1]
     is_top = gy == g_y - 1
     barrier = pltpu.get_barrier_semaphore()
 
@@ -217,15 +237,20 @@
 
 
 def conv_kernel(
-    g_y, g_x, fold_ref, inp_ref, cols_ref, from_ref, rs_ref, rn_ref, top_ref, mask_ref, w1_ref, w1s_ref, b1_ref, w2_ref,
+    g_y, g_x, fold_ref, state_ref, forcing_ref, cols_ref, from_ref, rs_ref, rn_ref, top_ref, mask_ref, w1_ref, w1s_ref, b1_ref, w2_ref,
     w2e_ref, b2_ref, sign_ref, out_ref, x_ref, far_ref, h_ref, north, south, edge, pedge, sem,
 ):
     gy, gx = lax.axis_index("gy"), lax.axis_index("gx")
     rows = out_ref.shape[0]
     hid = w1s_ref.shape[0]
     is_top = gy == g_y - 1
-    load = pltpu.make_async_copy(inp_ref, x_ref.at[pl.ds(2, rows)], sem)
-    load.start()
+    split = state_ref.shape[1]
+    loads = [
+        pltpu.make_async_copy(r, x_ref.at[pl.ds(2, rows), pl.ds(i * split, r.shape[1])], sem.at[i])
+        for i, r in enumerate((state_ref, forcing_ref))
+    ]
+    for load in loads:
+        load.start()
     lane256 = lax.broadcasted_iota(jnp.int32, (32, 256), 1)
     lane128 = lax.broadcasted_iota(jnp.int32, (32, 128), 1)
     back = (
@@ -297,7 +322,8 @@
     edge[0] = jnp.where(live, hidden_of(west_parts), 0.0)
     edge[1] = jnp.where(live, hidden_of(east_parts), 0.0)
 
-    load.wait()
+    for load in loads:
+        load.wait()
     for j in range(2):
         x_ref[j] = south[1, j].astype(bf16)
         x_ref[rows + 2 + j] = north[1, j].astype(bf16)
@@ -410,21 +436,32 @@
     incoming_rows = incoming[:, cap, 0, :cap].astype(jnp.int32)
     spread = np.zeros((block_cols, cols), np.float32)
     spread[np.arange(cols) // 2, np.arange(cols)] = 1
-    inputs, edge_cols = pl.pallas_call(
-        combine_kernel,
+    state, state_cols, state_ends = pl.pallas_call(
+        state_kernel,
         out_shape=(
-            jax.ShapeDtypeStruct((rows, cin, cols), bf16),
+            jax.ShapeDtypeStruct((rows, levels4, cols), bf16),
+            jax.ShapeDtypeStruct((2, tiles, levels4, 128), bf16),
+            jax.ShapeDtypeStruct((2, 2, levels4, cols), bf16),
+        ),
+        in_specs=[vmem()] * 2,
+        out_specs=(vmem(),) * 3,
+        compiler_params=params(),
+        cost_estimate=pl.CostEstimate(flops=rows * levels4 * cols * 8, bytes_accessed=rows * levels4 * cols * 4, transcendentals=0),
+        name="state",
+    )(ocean_state, land_mask)
+    forcing, edge_cols, ends = pl.pallas_call(
+        forcing_kernel,
+        out_shape=(
+            jax.ShapeDtypeStruct((rows, fields, cols), bf16),
             jax.ShapeDtypeStruct((2, tiles, cin, 128), bf16),
+            jax.ShapeDtypeStruct((2, 2, cin, cols), bf16),
         ),
-        in_specs=[smem()] + [vmem()] * 4,
-        out_specs=(vmem(), vmem()),
+        in_specs=[smem()] + [vmem()] * 5,
+        out_specs=(vmem(),) * 3,
         scratch_shapes=[pltpu.VMEM((half + 1, fields, block_cols), f32), pltpu.VMEM((half, fields, cols), f32)],
         compiler_params=params(),
-        name="combine",
-    )(
-        incoming_rows.reshape(slots), incoming, ocean_state, land_mask,
-        jnp.asarray(spread, bf16),
-    )
+        name="forcing",
+    )(incoming_rows.reshape(slots), incoming, land_mask, jnp.asarray(spread, bf16), state_cols, state_ends)
 
     from_cols, rows_s, rows_n, top_all = pl.pallas_call(
         functools.partial(exchange_kernel, g_y, g_x),
@@ -441,7 +478,7 @@
         ],
         compiler_params=pltpu.CompilerParams(collective_id=0, has_side_effects=True),
         name="exchange",
-    )(edge_cols, inputs)
+    )(edge_cols, ends)
 
     def band(r):
         t = np.zeros((3, r, r + 2), np.float32)
@@ -462,7 +499,7 @@
     return pl.pallas_call(
         functools.partial(conv_kernel, g_y, g_x),
         out_shape=jax.ShapeDtypeStruct((rows, outs, cols), bf16),
-        in_specs=[smem(), anym()] + [vmem()] * 13,
+        in_specs=[smem(), anym(), anym()] + [vmem()] * 13,
         out_specs=vmem(),
         scratch_shapes=[
             pltpu.VMEM(x_shape, bf16),
@@ -472,12 +509,12 @@
             pltpu.VMEM((3, 2, cin, cols), f32),
             pltpu.VMEM((2, hid, 128 * (tiles + 2)), f32),
             pltpu.VMEM((2, tiles + 2, outs, 128), f32),
-            pltpu.SemaphoreType.DMA,
+            pltpu.SemaphoreType.DMA((2,)),
         ],
         compiler_params=params(),
         name="conv",
     )(
-        fold_pair, inputs, edge_cols, from_cols, rows_s, rows_n, top_all, land_mask, w1, w1s, first_bias[:, None], w2,
+        fold_pair, state, forcing, edge_cols, from_cols, rows_s, rows_n, top_all, land_mask, w1, w1s, first_bias[:, None], w2,
         w2e, second_bias[:, None], signs,
     )
 

time: 109 us -> 103 us (0.945)
  waiting for transfers between devices: 31 us -> 22.2 us
  Pallas kernels: 61.3 us -> 63.8 us
    all_to_all x1, waiting for transfers between devices: 31 us -> 22.2 us  [per_device(): lax.all_to_all(outgoing, ('gy', 'gx'), split_axis=0, concat_axis=0, tiled...]
    pallas_call x1 -> x2, Pallas kernels: 17.8 us -> 19.6 us  [the longest x1 10.8 us: per_device(): pl.pallas_call(forcing_kernel, out_shape=(jax.ShapeDtypeStruct((rows, fie...]
  transfers between devices with their start and end apart: 1 -> 1, of which waited for: 1 -> 1; matrix products, arithmetic and copies ran while one was open for 8% -> 8% of each run, Pallas kernels for 0% -> 9%
where the time goes in v3:
time: 103 us; the launch traced here: 102 us
  Pallas kernels  63.8 us (62%)
  waiting for transfers between devices  22.2 us (22%)
  local copies, waits for them, and re-layouts  7.87 us (8%)
  starting transfers between devices  6.13 us (6%)
  other arithmetic  1.5 us (1%)
    pallas_call x1, Pallas kernels, per_device(): pl.pallas_call(functools.partial(conv_kernel, g_y, g_x), out_shape=jax.Sh...  28.1 us
    all_to_all x1, waiting for transfers between devices, per_device(): lax.all_to_all(outgoing, ('gy', 'gx'), split_axis=0, concat_axis=0, tiled...  22.2 us
    pallas_call x1, Pallas kernels, per_device(): pl.pallas_call(functools.partial(exchange_kernel, g_y, g_x), out_shape=(j...  12.6 us
    pallas_call x1, Pallas kernels, per_device(): pl.pallas_call(forcing_kernel, out_shape=(jax.ShapeDtypeStruct((rows, fie...  10.8 us
    pallas_call x1, Pallas kernels, per_device(): pl.pallas_call(state_kernel, out_shape=(jax.ShapeDtypeStruct((rows, level...  8.77 us
    all_to_all x1, starting transfers between devices, per_device(): lax.all_to_all(outgoing, ('gy', 'gx'), split_axis=0, concat_axis=0, tiled...  6.13 us
    reshape x2, local copies, waits for them, and re-layouts, per_device(): jnp.einsum('urs,uvoc->vrosc', band(R1), first_weight)  4.01 us
    pallas_call x1, Pallas kernels, per_device(): pl.pallas_call(functools.partial(pack_kernel, empty=half), out_shape=jax....  3.54 us
  transfers between devices with their start and end apart: 1, of which 1 were waited for; matrix products, arithmetic and copies ran while one was open for 8% of the time, Pallas kernels for 9%

profile of v3, /device:TPU:6, one launch (start us, length us, event | category | flops | bytes accessed | tf_op | source)
XLA Modules:
  0.0 102.3 jit_solution(5502149040373417690)
XLA Ops:
  0.0 3.5 %pack.1 = bf16[32,13,16,128]{3,2,1,0:T(8,128)(2,1)} custom-call(s32[192]{0:T(256)} %bitcast.34, s32[192]{0:T(256)} %row_ref.1, s32[192]{0:T(256)} %live_ref.1, bf16[192,16,128]{2,1,0:T(8,128)(2,1)} %atm_ref.1), custom_call_target="tpu_custom_call" | custom-call | tf_op jit(solution)/shard_map/pack/pallas_call | solution.py:427
  3.6 0.0 copy-start.2
  3.6 6.1 %all-to-all-start = ((bf16[32,13,16,128]{3,2,1,0:T(8,128)(2,1)}), bf16[32,13,16,128]{3,2,1,0:T(8,128)(2,1)}, u32[]{:S(2)}, u32[]{:S(2)}) async-start(bf16[32,13,16,128]{3,2,1,0:T(8,128)(2,1)} %pack.1), calls=%async_computation | async-start | bytes 3407872 | tf_op jit(solution)/shard_map/all_to_all | solution.py:435
  9.7 0.0 copy-done.4
  9.7 0.7 copy.34.b2_ref
  10.4 0.1 stack_reshape.6
  10.5 0.1 stack_reshape.7
  10.6 0.0 copy-done.3
  10.6 0.7 copy.33.b1_ref
  11.3 0.0 copy-done
  11.3 0.7 copy.32.w1s_ref
  12.0 0.3 convolution_bitcast_fusion.1
  12.3 0.9 reshape.19.w2_ref
  13.2 0.5 convolution_bitcast_fusion
  13.7 1.6 %copy.36 = bf16[3,6,64,8,32]{4,3,2,1,0:T(8,128)(2,1)S(1)} copy(bf16[3,6,64,8,32]{2,3,4,0,1:T(8,128)(2,1)S(1)} %convolution_bitcast_fusion) | data formatting | bytes 1179648 | tf_op jit(solution)/shard_map/reshape | solution.py:489
  15.3 2.4 %reshape.24.w1_ref = bf16[3,384,256]{2,1,0:T(8,128)(2,1)} reshape(bf16[3,6,64,8,32]{4,3,2,1,0:T(8,128)(2,1)S(1)} %copy.36) | data formatting | bytes 1179648 | tf_op jit(solution)/shard_map/reshape | solution.py:489
  17.7 8.8 %state.1 = (bf16[384,16,256]{2,1,0:T(8,128)(2,1)}, bf16[2,6,16,128]{3,2,1,0:T(8,128)(2,1)}, bf16[2,2,16,256]{3,2,1,0:T(8,128)(2,1)}) custom-call(bf16[384,16,256]{2,1,0:T(8,128)(2,1)} %state_ref.1, s32[384,256]{1,0:T(8,128)} %mask_ref.5), custom_call_target="tpu_custom_call" | custom-call | flops 12582912 | bytes 6291456 | tf_op jit(solution)/shard_map/state/pallas_call | solution.py:439
  26.5 0.6 pad_maximum_fusion.w2e_ref
  27.1 22.2 %all-to-all-done.blocks_ref = bf16[32,13,16,128]{3,2,1,0:T(8,128)(2,1)} async-done(((bf16[32,13,16,128]{3,2,1,0:T(8,128)(2,1)}), bf16[32,13,16,128]{3,2,1,0:T(8,128)(2,1)}, u32[]{:S(2)}, u32[]{:S(2)}) %all-to-all-start) | async-done | bytes 1703968 | tf_op jit(solution)/shard_map/all_to_all | solution.py:435
  49.3 0.9 fusion.4
  50.2 0.7 reshape.20.rows_ref
  50.9 10.8 %forcing.1 = (bf16[384,16,256]{2,1,0:T(8,128)(2,1)}, bf16[2,6,32,128]{3,2,1,0:T(8,128)(2,1)}, bf16[2,2,32,256]{3,2,1,0:T(8,128)(2,1)}) custom-call(s32[384]{0:T(512)} %reshape.20.rows_ref, bf16[32,13,16,128]{3,2,1,0:T(8,128)(2,1)} %all-to-all-done.blocks_ref, s32[384,256]{1,0:T(8,128)} %mask_ref.5, bf16[128,256]{1,0:T(8,128)(2,1)} %constant.6.clone.up_ref, ...), custom_call_target="tpu_custom_call" | custom-call | tf_op jit(solution)/shard_map/forcing/pallas_call | solution.py:452
  61.7 12.6 %exchange.1 = (bf16[2,6,32,128]{3,2,1,0:T(8,128)(2,1)}, bf16[3,2,32,256]{3,2,1,0:T(8,128)(2,1)}, bf16[3,2,32,256]{3,2,1,0:T(8,128)(2,1)}, bf16[8,2,32,256]{3,2,1,0:T(8,128)(2,1)}) custom-call(bf16[2,6,32,128]{3,2,1,0:T(8,128)(2,1)} %get-tuple-element.19.cols_ref, bf16[2,2,32,256]{3,2,1,0:T(8,128)(2,1)} %get-tuple-element.20.ends_ref), custom_call_target="tpu_custom_call" | custom-call | tf_op jit(solution)/shard_map/exchange/pallas_call | solution.py:466
  74.3 28.1 %conv.1 = bf16[384,8,256]{2,1,0:T(8,128)(2,1)} custom-call(s32[8]{0:T(128)} %fold_ref.1, bf16[384,16,256]{2,1,0:T(8,128)(2,1)} %get-tuple-element.15.state_ref, bf16[384,16,256]{2,1,0:T(8,128)(2,1)} %get-tuple-element.18.forcing_ref, bf16[2,6,32,128]{3,2,1,0:T(8,128)(2,1)} %get-tuple-element.19.cols_ref, bf16[2,6,32,128]{3,2,1,0:T(8,128)(2,1)} %get-tuple-element.21.from_ref, ...), custom_call_target="tpu_custom_call" | custom-call | tf_op jit(solution)/shard_map/conv/pallas_call | solution.py:499
  (10 shorter events, 0.0 us)
Async XLA Ops:
  3.5 6.2 %copy-start.4 = (f32[8]{0:T(128)S(1)}, f32[8]{0:T(128)}, u32[]{:S(2)}) copy-start(f32[8]{0:T(128)} %param.25) | copy-start | bytes 100
  3.5 6.8 %copy-start.1 = (bf16[3,3,8,64]{3,2,1,0:T(8,128)(2,1)S(1)}, bf16[3,3,8,64]{3,2,1,0:T(8,128)(2,1)}, u32[]{:S(2)}) copy-start(bf16[3,3,8,64]{3,2,1,0:T(8,128)(2,1)} %param.24) | copy-start | bytes 27652
  3.5 7.0 %copy-start.3 = (f32[64]{0:T(128)S(1)}, f32[64]{0:T(128)}, u32[]{:S(2)}) copy-start(f32[64]{0:T(128)} %param.23) | copy-start | bytes 772
  3.5 7.7 %copy-start = (bf16[3,3,64,32]{2,3,1,0:T(8,128)(2,1)S(1)}, bf16[3,3,64,32]{2,3,1,0:T(8,128)(2,1)}, u32[]{:S(2)}) copy-start(bf16[3,3,64,32]{2,3,1,0:T(8,128)(2,1)} %param.22) | copy-start | bytes 110596
  3.6 8.4 %copy-start.2 = (bf16[3,6,8,1,1]{2,0,4,3,1:T(4,128)(2,1)S(1)}, bf16[3,6,8,1,1]{2,0,4,3,1:T(4,128)(2,1)}, u32[]{:S(2)}) copy-start(bf16[3,6,8,1,1]{2,0,4,3,1:T(4,128)(2,1)} %constant.9) | copy-start | bytes 868
  3.6 45.7 %all-to-all-start = ((bf16[32,13,16,128]{3,2,1,0:T(8,128)(2,1)}), bf16[32,13,16,128]{3,2,1,0:T(8,128)(2,1)}, u32[]{:S(2)}, u32[]{:S(2)}) async-start(bf16[32,13,16,128]{3,2,1,0:T(8,128)(2,1)} %pack.1), calls=%async_computation | async-start | bytes 3407872 | tf_op jit(solution)/shard_map/all_to_all | solution.py:435
